TPU v7x, 32 devices: a whole 2x2x4 slice. The times are simulated.
32 devices in a mesh: dp: 16 (over z, y, core), tensor: 2 (over x).
Axes of the slice: x: 2, y: 2, z: 4, core: 2. Of those that a mesh axis runs over, the one named last changes fastest.
Arguments:
- x_in: bfloat16 [32768, 768], P(('dp', 'tensor')), may hold values from -6 to 6
- cotangent: bfloat16 [32768, 768], P(('dp', 'tensor')), may hold values from -6 to 6
- sequence_lengths: int32 [32], replicated, may hold values from 1 to 2047, as said below
- sequence_owner: int32 [32], replicated, may hold values from 0 to 15, as said below
- norm_gain: float32 [768], replicated, may hold values from 0.5 to 1.5
- proj_gate: bfloat16 [768, 1536], P('dp', 'tensor'), may hold values from -0.21875 to 0.21875
- proj_value: bfloat16 [768, 1536], P('dp', 'tensor'), may hold values from -0.21875 to 0.21875
- proj_bc: bfloat16 [768, 256], P('dp'), may hold values from -0.21875 to 0.21875
- proj_step: bfloat16 [768, 24], P('dp', 'tensor'), may hold values from -0.21875 to 0.21875
- proj_out: bfloat16 [1536, 768], P('tensor', 'dp'), may hold values from -0.15625 to 0.15625
- conv_value: float32 [4, 1536], P(None, 'tensor'), may hold values from -3 to 3
- conv_value_bias: float32 [1536], P('tensor'), may hold values from -1.5 to 1.5
- conv_bc: float32 [4, 256], replicated, may hold values from -3 to 3
- conv_bc_bias: float32 [256], replicated, may hold values from -1.5 to 1.5
- step_bias: float32 [24], P('tensor'), may hold values from -5 to -1
- decay_log: float32 [24], P('tensor'), may hold values from 0 to 2.77
- skip_gain: float32 [24], P('tensor'), may hold values from 0.1 to 1.9
- gate_gain: float32 [1536], P('tensor'), may hold values from 0.5 to 1.5
Outputs:
- block_out: bfloat16 [32768, 768], P(('dp', 'tensor'))
- grad_in: bfloat16 [32768, 768], P(('dp', 'tensor'))
- g_norm_gain: float32 [768], replicated
- g_proj_gate: float32 [768, 1536], P('dp', 'tensor')
- g_proj_value: float32 [768, 1536], P('dp', 'tensor')
- g_proj_bc: float32 [768, 256], P('dp')
- g_proj_step: float32 [768, 24], P('dp', 'tensor')
- g_proj_out: float32 [1536, 768], P('tensor', 'dp')
- g_conv_value: float32 [4, 1536], P(None, 'tensor')
- g_conv_value_bias: float32 [1536], P('tensor')
- g_conv_bc: float32 [4, 256], replicated
- g_conv_bc_bias: float32 [256], replicated
- g_step_bias: float32 [24], P('tensor')
- g_decay_log: float32 [24], P('tensor')
- g_skip_gain: float32 [24], P('tensor')
- g_gate_gain: float32 [1536], P('tensor')
Inputs may be any that keep to these rules, and one draw needn't show every extreme that they name: `sequence_owner`: each index of dp owns exactly 2 sequences. `sequence_lengths`: the lengths of the sequences of one index of dp sum to at most 2048, and to exactly 2048 for some index.
All inputs are finite; a program needn't handle non-finite values.
Results may differ from a plain program's by a relative error of at most 0.0095.
Values may be sent and summed in bfloat16 or wider, within the bound.
A program may use at most 192 MiB of HBM per device.

v0:
```python
from functools import partial

import jax
import jax.numpy as jnp
from jax import lax
from jax.sharding import PartitionSpec as P

BLOCK = 256


EPSILON = 1e-05
PRECISION = lax.Precision.HIGHEST


def segments(sequence_lengths, sequence_owner, device, row_count):
    owned = (sequence_owner == device).astype(jnp.int32)
    seq_ends = jnp.cumsum(sequence_lengths * owned, dtype=jnp.int32)
    positions = jnp.arange(row_count, dtype=jnp.int32)
    finished = (seq_ends[None, :] <= positions[:, None]) & (owned[None, :] == 1)
    segment = jnp.sum(finished.astype(jnp.int32), axis=1, dtype=jnp.int32)
    present = positions < seq_ends[-1]
    return (segment, present)


def conv_seq(values, kernel, offset_bias, segment):
    kernel_size = kernel.shape[0]
    row_count = values.shape[0]
    result = offset_bias + kernel[kernel_size - 1] * values
    for offset in range(1, kernel_size):
        moved = jnp.pad(values[: row_count - offset], ((offset, 0), (0, 0)))
        before = jnp.pad(segment[: row_count - offset], (offset, 0), constant_values=-1)
        result = (
            result
            + kernel[kernel_size - 1 - offset]
            * moved
            * (before == segment).astype(jnp.float32)[:, None]
        )
    return result


def scan_heads(values, keys_b, query_c, step_size, decay_rate, segment):
    row_count, head_count, head_dim = values.shape
    state_size = keys_b.shape[1]
    blocks = row_count // BLOCK
    value_blocks = values.reshape(blocks, BLOCK, head_count, head_dim)
    step_blocks = step_size.reshape(blocks, BLOCK, head_count)
    key_blocks = keys_b.reshape(blocks, BLOCK, state_size)
    query_blocks = query_c.reshape(blocks, BLOCK, state_size)
    segment_blocks = segment.reshape(blocks, BLOCK)
    lower_mask = jnp.arange(BLOCK)[:, None] >= jnp.arange(BLOCK)[None, :]
    rates = step_blocks * decay_rate
    cum_rates = jnp.einsum(
        "ij,cjh->cih", lower_mask.astype(jnp.float32), rates, precision=PRECISION
    )
    same_segment = lower_mask[None] & (segment_blocks[:, :, None] == segment_blocks[:, None, :])
    rate_gaps = cum_rates[:, :, None, :] - cum_rates[:, None, :, :]
    decays = (
        jnp.exp(jnp.where(same_segment[..., None], rate_gaps, 0.0))
        * same_segment.astype(jnp.float32)[..., None]
    )
    scores = jnp.einsum("cin,cjn->cij", query_blocks, key_blocks, precision=PRECISION)
    score_weights = scores[..., None] * decays * step_blocks[:, None, :, :]
    inside = jnp.einsum("cijh,cjhp->cihp", score_weights, value_blocks, precision=PRECISION)
    last_rate = cum_rates[:, -1, :]
    tail_mask = (segment_blocks == segment_blocks[:, -1:]).astype(jnp.float32)
    tail_weight = jnp.exp(last_rate[:, None, :] - cum_rates) * tail_mask[..., None] * step_blocks
    states = jnp.einsum(
        "cjh,cjhp,cjn->chpn", tail_weight, value_blocks, key_blocks, precision=PRECISION
    )
    prev_last = jnp.concatenate([jnp.full((1,), -2, jnp.int32), segment_blocks[:-1, -1]])
    keep_flag = (segment_blocks[:, -1] == prev_last).astype(jnp.float32)
    carry_gain = jnp.exp(last_rate) * keep_flag[:, None]

    def advance(carry_state, block_item):
        gain_now, fresh_state = block_item
        return (gain_now[:, None, None] * carry_state + fresh_state, carry_state)

    ended, prior_state = lax.scan(
        advance, jnp.zeros((head_count, head_dim, state_size), jnp.float32), (carry_gain, states)
    )
    head_same = (segment_blocks == prev_last[:, None]).astype(jnp.float32)
    carried = jnp.einsum("cin,chpn->cihp", query_blocks, prior_state, precision=PRECISION)
    carried = carried * (jnp.exp(cum_rates) * head_same[..., None])[..., None]
    return (inside + carried).reshape(row_count, head_count, head_dim)


def mixer(
    value_proj,
    bc_proj,
    step_raw,
    conv_value,
    conv_value_bias,
    conv_bc,
    conv_bc_bias,
    step_bias,
    decay_log,
    skip_gain,
    segment,
):
    conv_out = jax.nn.silu(conv_seq(value_proj, conv_value, conv_value_bias, segment))
    bc_conv = jax.nn.silu(conv_seq(bc_proj, conv_bc, conv_bc_bias, segment))
    state_size = bc_proj.shape[1] // 2
    step_size = jax.nn.softplus(step_raw + step_bias)
    decay_rate = -jnp.exp(decay_log)
    row_count = value_proj.shape[0]
    head_count = step_size.shape[1]
    head_dim = value_proj.shape[1] // head_count
    values = conv_out.reshape(row_count, head_count, head_dim)
    mixed_out = scan_heads(
        values, bc_conv[:, :state_size], bc_conv[:, state_size:], step_size, decay_rate, segment
    )
    mixed_out = mixed_out + skip_gain[None, :, None] * values
    return mixed_out.reshape(row_count, head_count * head_dim)


def assemble(gathered):
    gate_full, value_full, bc_full, step_full, out_full = gathered
    in_weight = jnp.concatenate([gate_full, value_full, step_full, bc_full], 1)
    return (in_weight, out_full)


def contract_rows(left_side, right_side):
    return lax.dot_general(
        left_side, right_side, (((0,), (0,)), ((), ())), preferred_element_type=jnp.float32
    )


def contract_cols(left_side, right_side):
    return lax.dot_general(
        left_side, right_side, (((1,), (1,)), ((), ())), preferred_element_type=jnp.float32
    )


def widen(local_part, tensor_count, tensor_index):
    axis_last = local_part.ndim - 1
    width_local = local_part.shape[axis_last]
    shape_full = local_part.shape[:axis_last] + (width_local * tensor_count,)
    return lax.dynamic_update_slice_in_dim(
        jnp.zeros(shape_full, jnp.float32), local_part, tensor_index * width_local, axis_last
    )


def narrow(full_part, width_local, tensor_index):
    axis_last = full_part.ndim - 1
    return lax.dynamic_slice_in_dim(full_part, tensor_index * width_local, width_local, axis_last)


def body(
    x_in,
    cotangent,
    sequence_lengths,
    sequence_owner,
    norm_gain,
    proj_gate,
    proj_value,
    proj_bc,
    proj_step,
    proj_out,
    conv_value,
    conv_value_bias,
    conv_bc,
    conv_bc_bias,
    step_bias,
    decay_log,
    skip_gain,
    gate_gain,
):
    half_rows = x_in.shape[0]
    tensor_count = lax.axis_size("tensor")
    row_count = half_rows * tensor_count
    tensor_index = lax.axis_index("tensor")
    device_index = lax.axis_index("dp")
    inner_local = proj_gate.shape[1]
    heads_local = proj_step.shape[1]
    main_cols = 2 * inner_local + heads_local
    inner_all = inner_local * tensor_count
    in_float = x_in.astype(jnp.float32)
    in_rstd = lax.rsqrt(jnp.mean(in_float * in_float, axis=-1, keepdims=True) + EPSILON)
    in_hat = in_float * in_rstd
    normed = (in_hat * norm_gain).astype(jnp.bfloat16)
    gathered = (
        lax.all_gather(proj_gate, "dp", axis=0, tiled=True),
        lax.all_gather(proj_value, "dp", axis=0, tiled=True),
        lax.all_gather(proj_bc, "dp", axis=0, tiled=True),
        lax.all_gather(proj_step, "dp", axis=0, tiled=True),
        lax.all_gather(proj_out, "dp", axis=1, tiled=True),
    )
    in_weight, out_weight = assemble(gathered)
    normed_all = lax.all_gather(normed, "tensor", axis=0, tiled=True)
    projected = jnp.dot(normed_all, in_weight, preferred_element_type=jnp.float32)
    gate_z = projected[:, :inner_local]
    value_proj = projected[:, inner_local : 2 * inner_local]
    step_raw = projected[:, 2 * inner_local : main_cols]
    bc_proj = projected[:, main_cols:]
    segment, present = segments(sequence_lengths, sequence_owner, device_index, row_count)
    present_float = present.astype(jnp.float32)
    mixed_out, mixer_back = jax.vjp(
        jax.checkpoint(partial(mixer, segment=segment)),
        value_proj,
        bc_proj,
        step_raw,
        conv_value,
        conv_value_bias,
        conv_bc,
        conv_bc_bias,
        step_bias,
        decay_log,
        skip_gain,
    )
    gate_sigmoid = jax.nn.sigmoid(gate_z)
    silu_gate = gate_z * gate_sigmoid
    gated_out = mixed_out * silu_gate
    squares = lax.psum(jnp.sum(gated_out * gated_out, axis=-1), "tensor")
    gate_scale = lax.rsqrt(squares / inner_all + EPSILON)[:, None]
    gnorm = (gated_out * gate_scale * gate_gain).astype(jnp.bfloat16)
    branch_own = lax.psum_scatter(
        jnp.dot(gnorm, out_weight, preferred_element_type=jnp.float32).astype(jnp.bfloat16),
        "tensor",
        scatter_dimension=0,
        tiled=True,
    ).astype(jnp.float32)
    present_own = lax.dynamic_slice_in_dim(present_float, tensor_index * half_rows, half_rows, 0)
    block_out = (in_float + present_own[:, None] * branch_own).astype(jnp.bfloat16)
    back_in_weight, back_out_weight = (in_weight, out_weight)
    mask_rows = present_float.astype(jnp.bfloat16)
    masked_cot = lax.all_gather(cotangent, "tensor", axis=0, tiled=True) * mask_rows[:, None]
    part_rows = contract_cols(masked_cot, back_out_weight)
    grad_weight = contract_rows(gnorm, masked_cot)
    gated_scaled = gated_out * gate_scale
    grad_gate_gain = jnp.sum(part_rows * gated_scaled, axis=0)
    grad_hat = part_rows * gate_gain
    dot_sums = lax.psum(jnp.sum(grad_hat * gated_out, axis=-1), "tensor")
    grad_gated = (
        gate_scale * grad_hat
        - gated_out * (gate_scale * gate_scale * gate_scale) * (dot_sums / inner_all)[:, None]
    )
    grad_mixed = grad_gated * silu_gate
    grad_gate_z = grad_gated * mixed_out * gate_sigmoid * (1.0 + gate_z * (1.0 - gate_sigmoid))
    (
        grad_value,
        grad_bc_part,
        grad_step,
        g_conv_value,
        g_conv_value_bias,
        g_conv_bc,
        g_conv_bc_bias,
        g_step_bias,
        g_decay_log,
        g_skip_gain,
    ) = mixer_back(grad_mixed)
    grad_bc = lax.psum(grad_bc_part.astype(jnp.bfloat16), "tensor")
    grad_main = jnp.concatenate([grad_gate_z, grad_value, grad_step], 1).astype(jnp.bfloat16)
    main_weight = back_in_weight[:, :main_cols]
    bc_weight = back_in_weight[:, main_cols:]
    bc_own = lax.dynamic_slice_in_dim(grad_bc, tensor_index * half_rows, half_rows, 0)
    grad_normed = lax.psum_scatter(
        contract_cols(grad_main, main_weight).astype(jnp.bfloat16),
        "tensor",
        scatter_dimension=0,
        tiled=True,
    ).astype(jnp.float32) + contract_cols(bc_own, bc_weight)
    weight_main = contract_rows(normed_all, grad_main)
    weight_bc = contract_rows(normed_all, grad_bc)
    summed = (
        lax.psum_scatter(weight_main[:, :inner_local], "dp", scatter_dimension=0, tiled=True),
        lax.psum_scatter(
            weight_main[:, inner_local : 2 * inner_local], "dp", scatter_dimension=0, tiled=True
        ),
        lax.psum_scatter(weight_bc, "dp", scatter_dimension=0, tiled=True),
        lax.psum_scatter(weight_main[:, 2 * inner_local :], "dp", scatter_dimension=0, tiled=True),
        lax.psum_scatter(grad_weight, "dp", scatter_dimension=1, tiled=True),
    )
    grad_hat_in = grad_normed * norm_gain
    grad_in = in_rstd * (
        grad_hat_in - in_hat * jnp.mean(grad_hat_in * in_hat, axis=-1, keepdims=True)
    )
    grad_in = (grad_in + cotangent.astype(jnp.float32)).astype(jnp.bfloat16)
    gain_part = jnp.sum(grad_normed * in_hat, axis=0)
    small = lax.psum(
        (
            gain_part,
            g_conv_bc,
            g_conv_bc_bias,
            widen(g_conv_value, tensor_count, tensor_index),
            widen(g_conv_value_bias, tensor_count, tensor_index),
            widen(g_step_bias, tensor_count, tensor_index),
            widen(g_decay_log, tensor_count, tensor_index),
            widen(g_skip_gain, tensor_count, tensor_index),
            widen(grad_gate_gain, tensor_count, tensor_index),
        ),
        ("dp", "tensor"),
    )
    return (
        block_out,
        grad_in,
        small[0],
        summed[0],
        summed[1],
        summed[2],
        summed[3],
        summed[4],
        narrow(small[3], inner_local, tensor_index),
        narrow(small[4], inner_local, tensor_index),
        small[1],
        small[2],
        narrow(small[5], heads_local, tensor_index),
        narrow(small[6], heads_local, tensor_index),
        narrow(small[7], heads_local, tensor_index),
        narrow(small[8], inner_local, tensor_index),
    )


def solution(mesh):
    in_specs = (
        P(("dp", "tensor"), None),
        P(("dp", "tensor"), None),
        P(),
        P(),
        P(),
        P("dp", "tensor"),
        P("dp", "tensor"),
        P("dp", None),
        P("dp", "tensor"),
        P("tensor", "dp"),
        P(None, "tensor"),
        P("tensor"),
        P(),
        P(),
        P("tensor"),
        P("tensor"),
        P("tensor"),
        P("tensor"),
    )
    out_specs = (
        P(("dp", "tensor"), None),
        P(("dp", "tensor"), None),
        P(),
        P("dp", "tensor"),
        P("dp", "tensor"),
        P("dp", None),
        P("dp", "tensor"),
        P("tensor", "dp"),
        P(None, "tensor"),
        P("tensor"),
        P(),
        P(),
        P("tensor"),
        P("tensor"),
        P("tensor"),
        P("tensor"),
    )
    return jax.shard_map(body, mesh=mesh, in_specs=in_specs, out_specs=out_specs, check_vma=False)
```

profile of v0, /device:TPU:0, one launch (start us, length us, event | category | flops | bytes accessed | tf_op | source)
XLA Modules:
  0.0 1068.3 jit_solution(10979998069129663397)
XLA Ops:
  20.2 23.3 %all-gather = bf16[16,48,12]{1,2,0:T(8,128)(2,1)S(1)} all-gather(bf16[1,48,12]{1,2,0:T(8,128)(2,1)S(1)} %bitcast.325), channel_id=1, replica_groups=mesh['dp'=16,'tensor'=2] {'dp'}, dimensions={0}, use_global_device_ids=true | all-gather | bytes 19584 | tf_op jit(solution)/shard_map/all_gather | solution.py:185
  43.7 18.8 %all_gather.25 = bf16[768,256]{1,0:T(8,128)(2,1)S(1)} all-gather(bf16[48,256]{1,0:T(8,128)(2,1)S(1)} %copy-done.85), channel_id=1, replica_groups=mesh['dp'=16,'tensor'=2] {'dp'}, dimensions={0}, use_global_device_ids=true | all-gather | bytes 417792 | tf_op jit(solution)/shard_map/all_gather | solution.py:184
  66.3 24.7 %all-gather.11.cloned.1.call-done = bf16[768,768]{1,0:T(8,128)(2,1)} async-done(((bf16[48,768]{1,0:T(8,128)(2,1)}), bf16[768,768]{1,0:T(8,128)(2,1)}) %all-gather.11.cloned.1.call-update) | async-done | bytes 1179664 | tf_op jit(solution)/shard_map/all_gather | solution.py:183
  91.1 5.4 concatenate.22
  96.5 40.7 %all-gather.7.cloned.1.call-done = bf16[2048,768]{1,0:T(8,128)(2,1)} async-done(((bf16[1024,768]{1,0:T(8,128)(2,1)}), bf16[2048,768]{1,0:T(8,128)(2,1)}) %all-gather.7.cloned.1.call-update) | async-done | bytes 3145744 | tf_op jit(solution)/shard_map/all_gather | solution.py:189
  137.1 8.7 fusion.173
  164.6 9.1 divide_multiply_fusion
  178.3 9.0 fusion.40
  189.5 27.5 %while.49 = (s32[]{:T(128)}, f32[12,64,128]{2,1,0:T(8,128)S(1)}, f32[8,12,64,128]{3,2,1,0:T(8,128)}, f32[8,12]{1,0:T(8,128)S(1)}, f32[8,12,64,128]{3,2,1,0:T(8,128)}, /*index=5*/s32[]{:T(128)}, s32[]{:T(128)}) while((s32[]{:T(128)}, f32[12,64,128]{2,1,0:T(8,128)S(1)}, f32[8,12,64,128]{3,2,1,0:T(8,128)}, f32[8,12]{1,0:T(8,128)S(1)}, ...), condition=%wide.region_4.5_spmd.clone, body=%wide.region_3.4_spmd.clone.sunk | while | flops 393219 | bytes 1966332 | solution.py:78
  220.4 35.0 %fusion.10 = f32[8,12,64,256]{3,2,1,0:T(8,128)S(1)} fusion(f32[8,256,12]{1,2,0:T(8,128)} %get-tuple-element.526, f32[8,256,256]{2,1,0:T(8,128)} %get-tuple-element.530, f32[8,256,12]{1,2,0:T(8,128)} %copy-done.44, f32[8,256,256]{2,1,0:T(8,128)S(1)} %fusion.97, pred[8,256,256]{2,1,0:T(8,128)(4,1)} %get-tuple-element.529, f32[8,256,12,64]{1,0,3,2:T(8,128)} %bitcast.279), kind=kOutput, calls=%fused_computation.25 | convolution fusion | flops 4863295488 | bytes 17498112 | tf_op jit(solution)/shard_map/jvp(cijh,cjhp->cihp)/dot_general | solution.py:63
  255.8 6.2 bitcast_add_fusion.4
  270.0 8.7 multiply_reduce_fusion.10
  278.8 5.0 psum.84
  283.8 10.9 %multiply_reduce_fusion.2 = (f32[768]{0:T(1024)}, f32[2048]{0:T(1024)S(1)}, f32[2048,768]{0,1:T(8,128)}) fusion(f32[2048,768]{0,1:T(8,128)} %get-tuple-element.494, f32[2048]{0:T(1024)S(1)} %get-tuple-element.539, f32[768]{0:T(1024)S(1)} %copy-done.108, bf16[768,768]{0,1:T(8,128)(2,1)} %all-gather.13.cloned.1.call-done, ...), kind=kOutput, calls=%fused_computation.61 | convolution fusion | flops 2426926336 | bytes 16934912 | tf_op jit(solution)/shard_map/dot_general | solution.py:129
  294.7 5.0 psum.85
  299.8 19.4 %multiply_convert_fusion = (bf16[2048,768]{0,1:T(8,128)(2,1)}, f32[2048,768]{0,1:T(8,128)}, f32[2048,768]{0,1:T(8,128)}) fusion(f32[2048,1804]{0,1:T(8,128)} %copy-done, f32[2048]{0:T(1024)S(1)} %broadcast_multiply_fusion.6, f32[2048,768]{0,1:T(8,128)} %get-tuple-element.494, f32[2048]{0:T(1024)S(1)} %get-tuple-element.538, ...), kind=kLoop, calls=%fused_computation.72 | loop fusion | flops 29884416 | bytes 53508096 | tf_op jit(solution)/shard_map/convert.2
  333.7 8.9 copy.277
  342.8 10.1 multiply_reduce_fusion.3
  359.6 9.2 fusion.50
  369.3 13.9 %while.50 = (s32[]{:T(128)}, f32[12,64,128]{2,1,0:T(8,128)S(1)}, f32[8,12,64,128]{3,2,1,0:T(8,128)S(1)}, f32[8,12,1,1]{1,3,2,0:T(1,128)}, f32[8,12]{1,0:T(8,128)...) while((s32[]{:T(128)}, f32[12,64,128]{2,1,0:T(8,128)S(1)}, ...), condition=%wide.region_11.12_spmd.clone, body=%wide.region_10.11_spmd.clone.sunk | while | flops 393219 | bytes 1966904 | solution.py:78
  383.2 11.7 %fusion.47 = f32[8,12,64,128]{3,2,1,0:T(8,128)} fusion(f32[8,256,128,1]{2,1,3,0:T(8,128)} %copy.235, f32[8,256,12,64]{1,0,3,2:T(8,128)} %bitcast.258, f32[8,256,12]{1,2,0:T(8,128)} %get-tuple-element.521), kind=kOutput, calls=%fused_computation.89 | convolution fusion | flops 2417491968 | bytes 10584064 | tf_op jit(solution)/shard_map/transpose(jvp(jvp()))/checkpoint/cin,chpn->cihp/dot_general | solution.py:82
  395.0 7.7 multiply_reduce_fusion.8
  402.6 11.9 %fusion.94 = f32[8,256,128]{2,1,0:T(8,128)} fusion(f32[8,12,64,128]{3,2,1,0:T(8,128)S(1)} %get-tuple-element.725, f32[8,256,12,64]{1,0,3,2:T(8,128)S(1)} %bitcast.263, f32[8,256,12]{1,2,0:T(8,128)S(1)} %copy-done.40), kind=kOutput, calls=%fused_computation.155 | convolution fusion | flops 2417491968 | bytes 10584064 | tf_op jit(solution)/shard_map/transpose(jvp(jvp()))/checkpoint/cin,chpn->cihp/dot_general | solution.py:82
  416.7 21.4 %while.51 = (s32[]{:T(128)}, f32[12,64,128]{2,1,0:T(8,128)S(1)}, f32[8,12]{1,0:T(8,128)S(1)}, f32[8,12,64,128]{3,2,1,0:T(8,128)}, f32[8,12,64,128]{3,2,1,0:T(8,1...) while((s32[]{:T(128)}, f32[12,64,128]{2,1,0:T(8,128)S(1)}, ...), condition=%wide.region_14.15_spmd.clone, body=%wide.region_12.14_spmd.clone.sunk | while | flops 589816 | bytes 2359732 | solution.py:78
  438.1 16.0 %fusion.93 = f32[8,256,128]{2,1,0:T(8,128)} fusion(f32[8,12,64,128]{3,2,1,0:T(8,128)} %get-tuple-element.263, f32[8,256,12,64]{1,0,3,2:T(8,128)} %bitcast.253, f32[8,256,12]{1,2,0:T(8,128)} %copy-done.38), kind=kOutput, calls=%fused_computation.154 | convolution fusion | flops 2417491968 | bytes 10584064 | tf_op jit(solution)/shard_map/transpose(jvp(jvp()))/checkpoint/cjh,cjhp,cjn->chpn/dot_general | solution.py:67
  454.1 7.3 fusion.174
  464.2 9.2 multiply_reduce_fusion.1
  476.9 48.5 %fusion.18 = (f32[8,256,12]{1,2,0:T(8,128)}, f32[8,256,12]{1,2,0:T(8,128)}, f32[8,256,12]{1,2,0:T(8,128)}, f32[8,256,256]{2,1,0:T(8,128)}) fusion(f32[8,256,12]{1,2,0:T(8,128)S(1)} %get-tuple-element.525, f32[8,256,256]{2,1,0:T(8,128)S(1)} %copy-done.35, f32[8,256,12]{1,2,0:T(8,128)S(1)} %copy-done.34, f32[8,256,256]{2,1,0:T(8,128)} %fusion.175, ...), kind=kOutput, calls=%fused_computation.33 | convolution fusion | flops 4925612032 | bytes 19890176 | tf_op jit(solution)/shard_map/transpose(jvp(jvp()))/checkpoint/cijh,cjhp->cihp/dot_general | solution.py:63
  525.5 26.7 %bitcast_add_fusion.3 = f32[8,256,12,64]{1,3,2,0:T(8,128)} fusion(f32[8,256,12,64]{1,3,2,0:T(8,128)S(1)} %bitcast.274, f32[8,256,12]{1,2,0:T(8,128)S(1)} %copy-done.39, f32[8,256,12]{1,2,0:T(8,128)S(1)} %get-tuple-element.525, f32[8,256,256]{2,1,0:T(8,128)S(1)} %copy-done.35, f32[8,256,12]{1,2,0:T(8,128)S(1)} %copy-done.34, f32[8,256,256]{2,1,0:T(8,128)} %fusion.175, ...), kind=kOutput, calls=%fused_computation.55 | convolution fusion | flops 4866441216 | bytes 23887872 | tf_op jit(solution)/shard_map/transpose(jvp(jvp()))/checkpoint/cijh,cjhp->cihp/dot_general | solution.py:63
  552.3 5.5 convolution_add_fusion
  562.7 7.2 copy.217
  569.9 6.0 copy.281
  590.9 14.6 %multiply_reduce_fusion.7 = (f32[768]{0:T(1024)}, f32[2048,768]{0,1:T(8,128)}, f32[2048,768]{0,1:T(8,128)S(1)}) fusion(f32[2045,768]{0,1:T(8,128)} %bitcast.236, f32[2048]{0:T(1024)S(1)} %copy-done.52, f32[2048,768]{0,1:T(8,128)} %copy-done.6, f32[2048,768]{0,1:T(8,128)} %bitcast.280, f32[2048,768]{0,1:T(8,128)} %get-tuple-element.251, f32[768]{0:T(1024)S(1)} %mul.992), kind=kLoop, calls=%fused_computation.66 | loop fusion | flops 22019328 | bytes 37753856 | tf_op jit(solution)/shard_map/transpose(jvp(jvp()))/checkpoint/reduce_sum | solution.py:34
  605.5 7.2 slice_multiply_fusion.2
  612.7 6.5 multiply_reduce_fusion.6
  619.2 7.3 slice_multiply_fusion.1
  631.1 10.5 fusion.157
  641.6 8.7 fusion.78
  653.5 9.5 convolution_convert_fusion.1
  663.1 7.9 convolution_convert_fusion
  674.6 8.1 fusion.74
  713.4 40.7 %reduce-scatter.16.cloned.1.call-done = bf16[1024,768]{1,0:T(8,128)(2,1)} async-done(((bf16[2048,768]{1,0:T(8,128)(2,1)}), bf16[1024,768]{1,0:T(8,128)(2,1)}) %reduce-scatter.16.cloned.1.call-update) | async-done | bytes 1572880 | tf_op jit(solution)/shard_map/reduce_scatter | solution.py:256
  754.1 5.2 fusion.65
  759.3 41.4 %all-reduce.35 = (f32[768]{0:T(1024)}, f32[4,1536]{1,0:T(4,128)S(1)}, f32[1536]{0:T(1024)S(1)}, f32[4,256]{1,0:T(4,128)}, f32[256]{0:T(256)}, /*index=5*/f32[24]...) all-reduce(f32[768]{0:T(1024)} %get-tuple-element.416, ...), channel_id=1, replica_groups=mesh['dp'=16,'tensor'=2] {'dp','tensor'}, use_global_device_ids=true, to_apply=%region_25.26 | all-reduce | flops 11336 | bytes 90688 | tf_op jit(solution)/shard_map/psum | solution.py:279
  809.3 52.3 %reduce-scatter.18.cloned.1.call-done = f32[48,256]{1,0:T(8,128)} async-done(((f32[768,256]{1,0:T(8,128)}), f32[48,256]{1,0:T(8,128)}) %reduce-scatter.18.cloned.1.call-update) | async-done | bytes 49168 | tf_op jit(solution)/shard_map/reduce_scatter | solution.py:269
  861.6 66.9 %reduce-scatter.20.cloned.1.call-done = f32[768,48]{0,1:T(8,128)} async-done(((f32[768,768]{0,1:T(8,128)}), f32[768,48]{0,1:T(8,128)}) %reduce-scatter.20.cloned.1.call-update) | async-done | bytes 147472 | tf_op jit(solution)/shard_map/reduce_scatter | solution.py:271
  928.5 66.2 %reduce-scatter.24.cloned.1.call-done = f32[48,768]{1,0:T(8,128)} async-done(((f32[768,768]{1,0:T(8,128)}), f32[48,768]{1,0:T(8,128)}) %reduce-scatter.24.cloned.1.call-update) | async-done | bytes 147472
  994.7 66.8 %reduce-scatter.22.cloned.1.call-done = f32[48,768]{1,0:T(8,128)} async-done(((f32[768,768]{1,0:T(8,128)}), f32[48,768]{1,0:T(8,128)}) %reduce-scatter.22.cloned.1.call-update) | async-done | bytes 147472
  (567 shorter events, 203.8 us)
Async XLA Ops:
  7.3 36.4 %copy-start.85 = (bf16[48,256]{1,0:T(8,128)(2,1)S(1)}, bf16[48,256]{1,0:T(8,128)(2,1)}, u32[]{:S(2)}) copy-start(bf16[48,256]{1,0:T(8,128)(2,1)} %param.31) | copy-start | bytes 73732
  7.3 59.1 %all-gather.9.cloned.1.call-start = ((), (), s32[]{:S(2)}) async-start(), calls=%async_computation.8 | async-start | bytes 1253376 | tf_op jit(solution)/shard_map/all_gather | solution.py:182
  8.0 83.1 %all-gather.11.cloned.1.call-start = ((), (), s32[]{:S(2)}) async-start(), calls=%async_computation.9 | async-start | bytes 1253376 | tf_op jit(solution)/shard_map/all_gather | solution.py:183
  8.8 128.4 %all-gather.7.cloned.1.call-start = ((), (), s32[]{:S(2)}) async-start(), calls=%async_computation.7 | async-start | bytes 4718592 | tf_op jit(solution)/shard_map/all_gather | solution.py:189
  14.2 269.6 %all-gather.13.cloned.1.call-start = ((), (), s32[]{:S(2)}) async-start(), calls=%async_computation.10 | async-start | bytes 1253376 | tf_op jit(solution)/shard_map/all_gather | solution.py:186
  14.8 269.0 %all-gather.15.cloned.1.call-start = ((), (), s32[]{:S(2)}) async-start(), calls=%async_computation.12 | async-start | bytes 4718592 | tf_op jit(solution)/shard_map/all_gather | solution.py:226
  15.4 655.9 %all-reduce.38.cloned.1.call-start = ((), (), s32[]{:S(2)}) async-start(), calls=%async_computation.14 | async-start | bytes 2097152 | tf_op jit(solution)/shard_map/psum | solution.py:251
  16.9 129.0 %copy-start.47 = (pred[256,256]{1,0:T(8,128)(4,1)}, pred[256,256]{1,0:T(8,128)(4,1)S(1)}, u32[]{:S(2)}) copy-start(pred[256,256]{1,0:T(8,128)(4,1)S(1)} %iota_compare_fusion) | copy-start | bytes 196612
  43.7 102.2 %copy-start.45 = (bf16[16,48,12]{2,1,0:T(8,128)(2,1)}, bf16[16,48,12]{2,1,0:T(8,128)(2,1)S(1)}, u32[]{:S(2)}) copy-start(bf16[16,48,12]{2,1,0:T(8,128)(2,1)S(1)} %copy.267) | copy-start | bytes 55300
  62.5 83.4 %copy-start.36 = (bf16[768,256]{1,0:T(8,128)(2,1)}, bf16[768,256]{1,0:T(8,128)(2,1)S(1)}, u32[]{:S(2)}) copy-start(bf16[768,256]{1,0:T(8,128)(2,1)S(1)} %all_gather.25) | copy-start | bytes 1179652
  145.9 18.6 %copy-start = (f32[2048,1804]{0,1:T(8,128)}, f32[2048,1804]{0,1:T(8,128)S(1)}, u32[]{:S(2)}) copy-start(f32[2048,1804]{0,1:T(8,128)S(1)} %fusion.173) | copy-start | bytes 44335108
  159.5 17.9 %copy-start.44 = (f32[8,256,12]{1,2,0:T(8,128)}, f32[8,256,12]{1,2,0:T(8,128)S(1)}, u32[]{:S(2)}) copy-start(f32[8,256,12]{1,2,0:T(8,128)S(1)} %convolution_bitcast_fusion.2) | copy-start | bytes 294916
  162.1 163.2 %copy-start.1 = (f32[2048,256]{0,1:T(8,128)}, f32[2048,256]{0,1:T(8,128)S(1)}, u32[]{:S(2)}) copy-start(f32[2048,256]{0,1:T(8,128)S(1)} %get-tuple-element.254) | copy-start | bytes 6291460
  220.4 35.0 %copy-start.22 = (f32[2048,128]{0,1:T(8,128)S(1)}, f32[2048,128]{0,1:T(8,128)}, u32[]{:S(2)}) copy-start(f32[2048,128]{0,1:T(8,128)} %get-tuple-element.514) | copy-start | bytes 3145732
  220.4 35.4 %copy-start.12 = (f32[8,12,64,128]{3,2,1,0:T(8,128)S(1)}, f32[8,12,64,128]{3,2,1,0:T(8,128)}, u32[]{:S(2)}) copy-start(f32[8,12,64,128]{3,2,1,0:T(8,128)} %get-tuple-element.248) | copy-start | bytes 9437188
  220.4 35.4 %copy-start.49 = (f32[8,256,12]{1,2,0:T(8,128)S(1)}, f32[8,256,12]{1,2,0:T(8,128)}, u32[]{:S(2)}) copy-start(f32[8,256,12]{1,2,0:T(8,128)} %get-tuple-element.523) | copy-start | bytes 294916
  283.8 15.9 %copy-start.81 = (f32[2048]{0:T(1024)}, f32[2048]{0:T(1024)S(1)}, u32[]{:S(2)}) copy-start(f32[2048]{0:T(1024)S(1)} %get-tuple-element.539) | copy-start | bytes 24580
  299.7 20.4 %copy-start.48 = (pred[256,256]{1,0:T(8,128)(4,1)S(1)}, pred[256,256]{1,0:T(8,128)(4,1)}, u32[]{:S(2)}) copy-start(pred[256,256]{1,0:T(8,128)(4,1)} %copy-done.47) | copy-start | bytes 196612
  299.7 22.2 %copy-start.130 = (f32[12]{0:T(128)S(1)}, f32[12]{0:T(128)}, u32[]{:S(2)}) copy-start(f32[12]{0:T(128)} %param.39) | copy-start | bytes 148
  299.7 22.2 %copy-start.88 = (f32[4,256]{1,0:T(4,128)S(1)}, f32[4,256]{1,0:T(4,128)}, u32[]{:S(2)}) copy-start(f32[4,256]{1,0:T(4,128)} %param.36) | copy-start | bytes 12292
  299.7 23.5 %copy-start.69 = (f32[4,768]{1,0:T(4,128)S(1)}, f32[4,768]{1,0:T(4,128)}, u32[]{:S(2)}) copy-start(f32[4,768]{1,0:T(4,128)} %param.34) | copy-start | bytes 36868
  299.7 24.1 %copy-start.41 = (f32[2048,12]{0,1:T(8,128)S(1)}, f32[2048,12]{0,1:T(8,128)}, u32[]{:S(2)}) copy-start(f32[2048,12]{0,1:T(8,128)} %get-tuple-element.256) | copy-start | bytes 294916
  299.7 24.1 %copy-start.104 = (f32[12]{0:T(128)S(1)}, f32[12]{0:T(128)}, u32[]{:S(2)}) copy-start(f32[12]{0:T(128)} %param.38) | copy-start | bytes 148
  299.7 25.5 %copy-start.118 = (f32[256]{0:T(256)S(1)}, f32[256]{0:T(256)}, u32[]{:S(2)}) copy-start(f32[256]{0:T(256)} %param.37) | copy-start | bytes 3076
  333.6 26.0 %copy-start.13 = (f32[8,256,128,1]{2,1,3,0:T(8,128)}, f32[8,256,128,1]{2,1,3,0:T(8,128)S(1)}, u32[]{:S(2)}) copy-start(f32[8,256,128,1]{2,1,3,0:T(8,128)S(1)} %copy.237) | copy-start | bytes 3145732
  438.1 16.0 %copy-start.9 = (f32[8,12,64,128]{3,2,1,0:T(8,128)S(1)}, f32[8,12,64,128]{3,2,1,0:T(8,128)}, u32[]{:S(2)}) copy-start(f32[8,12,64,128]{3,2,1,0:T(8,128)} %get-tuple-element.263) | copy-start | bytes 9437188
  438.1 16.0 %copy-start.14 = (f32[8,256,128,1]{2,1,3,0:T(8,128)S(1)}, f32[8,256,128,1]{2,1,3,0:T(8,128)}, u32[]{:S(2)}) copy-start(f32[8,256,128,1]{2,1,3,0:T(8,128)} %copy-done.13) | copy-start | bytes 3145732
  473.7 51.7 %slice-start.8 = ((s8[6291456]{0:T(1024)(128)(4,1)}), s8[4194304]{0:T(1024)(128)(4,1)S(1)}, s32[]{:S(2)}) async-start(s8[6291456]{0:T(1024)(128)(4,1)} %bitcast.264), calls=%async_computation.28 | async-start | bytes 8388608
  473.7 51.7 %slice-start.12 = ((s8[6291456]{0:T(1024)(128)(4,1)}), s8[4194304]{0:T(1024)(128)(4,1)S(1)}, s32[]{:S(2)}) async-start(s8[6291456]{0:T(1024)(128)(4,1)} %bitcast.273), calls=%async_computation.32 | async-start | bytes 8388608
  476.9 48.6 %slice-start.9 = ((s8[6291456]{0:T(1024)(128)(4,1)}), s8[2097152]{0:T(1024)(128)(4,1)S(1)}, s32[]{:S(2)}) async-start(s8[6291456]{0:T(1024)(128)(4,1)} %bitcast.264), calls=%async_computation.29 | async-start | bytes 4194304
  476.9 48.6 %slice-start.13 = ((s8[6291456]{0:T(1024)(128)(4,1)}), s8[2097152]{0:T(1024)(128)(4,1)S(1)}, s32[]{:S(2)}) async-start(s8[6291456]{0:T(1024)(128)(4,1)} %bitcast.273), calls=%async_computation.33 | async-start | bytes 4194304
  476.9 48.6 %copy-start.39 = (f32[8,256,12]{1,2,0:T(8,128)S(1)}, f32[8,256,12]{1,2,0:T(8,128)}, u32[]{:S(2)}) copy-start(f32[8,256,12]{1,2,0:T(8,128)} %copy-done.38) | copy-start | bytes 294916
  525.5 26.7 %copy-start.121 = (f32[12]{0:T(128)S(1)}, f32[12]{0:T(128)}, u32[]{:S(2)}) copy-start(f32[12]{0:T(128)} %param.40) | copy-start | bytes 148
  525.5 26.9 %copy-start.21 = (f32[8,256,128]{2,1,0:T(8,128)S(1)}, f32[8,256,128]{2,1,0:T(8,128)}, u32[]{:S(2)}) copy-start(f32[8,256,128]{2,1,0:T(8,128)} %copy.214) | copy-start | bytes 3145732
  588.4 24.3 %slice-start.2 = ((s8[6291456]{0:T(1024)(128)(4,1)}), s8[2097152]{0:T(1024)(128)(4,1)S(1)}, s32[]{:S(2)}) async-start(s8[6291456]{0:T(1024)(128)(4,1)} %bitcast.242), calls=%async_computation.22 | async-start | bytes 4194304
  590.8 121.2 %reduce-scatter.26.cloned.1.call-start = ((), (), s32[]{:S(2)}) async-start(), calls=%async_computation.19 | async-start | bytes 417792
  590.9 21.9 %slice-start.3 = ((s8[6291456]{0:T(1024)(128)(4,1)}), s8[4194304]{0:T(1024)(128)(4,1)S(1)}, s32[]{:S(2)}) async-start(s8[6291456]{0:T(1024)(128)(4,1)} %bitcast.242), calls=%async_computation.23 | async-start | bytes 8388608
  653.5 100.6 %reduce-scatter.16.cloned.1.call-start = ((), (), s32[]{:S(2)}) async-start(), calls=%async_computation.13 | async-start | bytes 4718592 | tf_op jit(solution)/shard_map/reduce_scatter | solution.py:256
  663.0 142.1 %reduce-scatter.14.cloned.1.call-start = ((), (), s32[]{:S(2)}) async-start(), calls=%async_computation.11 | async-start | bytes 4718592 | tf_op jit(solution)/shard_map/reduce_scatter | solution.py:216
  671.0 190.6 %reduce-scatter.18.cloned.1.call-start = ((), (), s32[]{:S(2)}) async-start(), calls=%async_computation.15 | async-start | bytes 835584 | tf_op jit(solution)/shard_map/reduce_scatter | solution.py:269
  674.5 254.0 %reduce-scatter.20.cloned.1.call-start = ((), (), s32[]{:S(2)}) async-start(), calls=%async_computation.16 | async-start | bytes 2506752 | tf_op jit(solution)/shard_map/reduce_scatter | solution.py:271
  682.7 312.0 %reduce-scatter.24.cloned.1.call-start = ((), (), s32[]{:S(2)}) async-start(), calls=%async_computation.18 | async-start | bytes 2506752
  687.6 66.5 %copy-start.11 = (bf16[1024,768]{1,0:T(8,128)(2,1)S(1)}, bf16[1024,768]{1,0:T(8,128)(2,1)}, u32[]{:S(2)}) copy-start(bf16[1024,768]{1,0:T(8,128)(2,1)} %param.24) | copy-start | bytes 4718596
  687.6 66.5 %copy-start.37 = (bf16[768,256]{1,0:T(8,128)(2,1)S(1)}, bf16[768,256]{1,0:T(8,128)(2,1)}, u32[]{:S(2)}) copy-start(bf16[768,256]{1,0:T(8,128)(2,1)} %copy-done.36) | copy-start | bytes 1179652
  687.6 66.5 %copy-start.80 = (f32[1024]{0:T(1024)S(1)}, f32[1024]{0:T(1024)}, u32[]{:S(2)}) copy-start(f32[1024]{0:T(1024)} %copy-done.79) | copy-start | bytes 12292
  690.8 370.7 %reduce-scatter.22.cloned.1.call-start = ((), (), s32[]{:S(2)}) async-start(), calls=%async_computation.17 | async-start | bytes 2506752
  693.9 111.2 %copy-start.25 = (bf16[1024,768]{1,0:T(8,128)(2,1)S(1)}, bf16[1024,768]{1,0:T(8,128)(2,1)}, u32[]{:S(2)}) copy-start(bf16[1024,768]{1,0:T(8,128)(2,1)} %param.25) | copy-start | bytes 4718596
  695.4 109.7 %dynamic-slice-start = ((f32[2048]{0:T(1024)}, s32[]{:T(128)}), f32[1024]{0:T(1024)S(1)}, s32[]{:S(2)}) async-start(f32[2048]{0:T(1024)} %copy-done.86, s32[]{:T(128)} %select_n.48), calls=%async_computation.36 | async-start | bytes 8704 | tf_op jit(solution)/shard_map/dynamic_slice | solution.py:222
  (114 other events, 787.1 us)
Sparse Core Ops, SparseCore 0:
  10.4 41.1 all-gather.8
  53.9 37.1 all-gather.10
  93.2 43.8 all-gather.6
  139.3 38.3 all-gather.12
  179.1 43.8 all-gather.14
  590.9 40.1 all-reduce.37
  653.6 55.8 reduce-scatter.25
  711.7 42.3 reduce-scatter.15
  756.4 44.7 reduce-scatter.13
  805.1 56.3 reduce-scatter.17
  866.4 62.0 reduce-scatter.19
  932.7 61.9 reduce-scatter.23
  999.5 61.9 reduce-scatter.21
where the time goes:
time: 1070 us
  waiting for transfers between devices  361 us (34%)
  matrix products  269 us (25%)
  other arithmetic  193 us (18%)
  local copies, waits for them, and re-layouts  122 us (11%)
  blocking collectives  93.4 us (9%)
  between operations  16.2 us (2%)
  loops' own time  12.7 us (1%)
    unnamed x16, waiting for transfers between devices  136 us
    dot_general x3, matrix products, scan_heads(): jnp.einsum('cijh,cjhp->cihp', score_weights, value_blocks, precision=PREC...  110 us
    reduce_scatter x1, waiting for transfers between devices, body(): lax.psum_scatter(grad_weight, 'dp', scatter_dimension=1, tiled=True)  66.9 us
    reduce_scatter x1, waiting for transfers between devices, body(): lax.psum_scatter(weight_bc, 'dp', scatter_dimension=0, tiled=True)  52.3 us
    unnamed x314, local copies, waits for them, and re-layouts  42.4 us
    dot_general x4, matrix products, scan_heads(): jnp.einsum('cjh,cjhp,cjn->chpn', tail_weight, value_blocks, key_blocks, p...  41.5 us
    psum x1, blocking collectives, body(): lax.psum((gain_part, g_conv_bc, g_conv_bc_bias, widen(g_conv_value, tenso...  41.4 us
    reduce_scatter x1, waiting for transfers between devices, body(): lax.psum_scatter(contract_cols(grad_main, main_weight).astype(jnp.bfloat1...  40.7 us
  transfers between devices with their start and end apart: 13, of which 7 were waited for; matrix products, arithmetic and copies ran while one was open for 26% of the time, Pallas kernels for 0%

commit v1 on v0

--- a/solution.py
+++ b/solution.py
@@ -9,7 +9,8 @@
 
 
 EPSILON = 1e-05
-PRECISION = lax.Precision.HIGHEST
+PRECISION = lax.Precision.DEFAULT
+SUM_PRECISION = lax.Precision.HIGHEST
 
 
 def segments(sequence_lengths, sequence_owner, device, row_count):
@@ -50,7 +51,7 @@
     lower_mask = jnp.arange(BLOCK)[:, None] >= jnp.arange(BLOCK)[None, :]
     rates = step_blocks * decay_rate
     cum_rates = jnp.einsum(
-        "ij,cjh->cih", lower_mask.astype(jnp.float32), rates, precision=PRECISION
+        "ij,cjh->cih", lower_mask.astype(jnp.float32), rates, precision=SUM_PRECISION
     )
     same_segment = lower_mask[None] & (segment_blocks[:, :, None] == segment_blocks[:, None, :])
     rate_gaps = cum_rates[:, :, None, :] - cum_rates[:, None, :, :]
@@ -111,12 +112,6 @@
     )
     mixed_out = mixed_out + skip_gain[None, :, None] * values
     return mixed_out.reshape(row_count, head_count * head_dim)
-
-
-def assemble(gathered):
-    gate_full, value_full, bc_full, step_full, out_full = gathered
-    in_weight = jnp.concatenate([gate_full, value_full, step_full, bc_full], 1)
-    return (in_weight, out_full)
 
 
 def contract_rows(left_side, right_side):
@@ -178,20 +173,18 @@
     in_rstd = lax.rsqrt(jnp.mean(in_float * in_float, axis=-1, keepdims=True) + EPSILON)
     in_hat = in_float * in_rstd
     normed = (in_hat * norm_gain).astype(jnp.bfloat16)
-    gathered = (
-        lax.all_gather(proj_gate, "dp", axis=0, tiled=True),
-        lax.all_gather(proj_value, "dp", axis=0, tiled=True),
-        lax.all_gather(proj_bc, "dp", axis=0, tiled=True),
-        lax.all_gather(proj_step, "dp", axis=0, tiled=True),
-        lax.all_gather(proj_out, "dp", axis=1, tiled=True),
-    )
-    in_weight, out_weight = assemble(gathered)
+    side_pack = jnp.concatenate([proj_value, proj_step, proj_bc], 1)
+    gate_pack = jnp.concatenate([proj_gate, proj_out.T], 1)
+    side_weight = lax.all_gather(side_pack, "dp", axis=0, tiled=True)
+    gate_pack = lax.all_gather(gate_pack, "dp", axis=0, tiled=True)
+    gate_weight = gate_pack[:, :inner_local]
+    out_weight = gate_pack[:, inner_local:]
     normed_all = lax.all_gather(normed, "tensor", axis=0, tiled=True)
-    projected = jnp.dot(normed_all, in_weight, preferred_element_type=jnp.float32)
-    gate_z = projected[:, :inner_local]
-    value_proj = projected[:, inner_local : 2 * inner_local]
-    step_raw = projected[:, 2 * inner_local : main_cols]
-    bc_proj = projected[:, main_cols:]
+    projected = jnp.dot(normed_all, side_weight, preferred_element_type=jnp.float32)
+    value_proj = projected[:, :inner_local]
+    step_raw = projected[:, inner_local : inner_local + heads_local]
+    bc_proj = projected[:, inner_local + heads_local :]
+    gate_z = jnp.dot(normed_all, gate_weight, preferred_element_type=jnp.float32)
     segment, present = segments(sequence_lengths, sequence_owner, device_index, row_count)
     present_float = present.astype(jnp.float32)
     mixed_out, mixer_back = jax.vjp(
@@ -214,18 +207,16 @@
     gate_scale = lax.rsqrt(squares / inner_all + EPSILON)[:, None]
     gnorm = (gated_out * gate_scale * gate_gain).astype(jnp.bfloat16)
     branch_own = lax.psum_scatter(
-        jnp.dot(gnorm, out_weight, preferred_element_type=jnp.float32).astype(jnp.bfloat16),
+        contract_cols(gnorm, out_weight).astype(jnp.bfloat16),
         "tensor",
         scatter_dimension=0,
         tiled=True,
     ).astype(jnp.float32)
     present_own = lax.dynamic_slice_in_dim(present_float, tensor_index * half_rows, half_rows, 0)
     block_out = (in_float + present_own[:, None] * branch_own).astype(jnp.bfloat16)
-    back_in_weight, back_out_weight = (in_weight, out_weight)
     mask_rows = present_float.astype(jnp.bfloat16)
     masked_cot = lax.all_gather(cotangent, "tensor", axis=0, tiled=True) * mask_rows[:, None]
-    part_rows = contract_cols(masked_cot, back_out_weight)
-    grad_weight = contract_rows(gnorm, masked_cot)
+    part_rows = jnp.dot(masked_cot, out_weight, preferred_element_type=jnp.float32)
     gated_scaled = gated_out * gate_scale
     grad_gate_gain = jnp.sum(part_rows * gated_scaled, axis=0)
     grad_hat = part_rows * gate_gain
@@ -248,27 +239,35 @@
         g_decay_log,
         g_skip_gain,
     ) = mixer_back(grad_mixed)
-    grad_bc = lax.psum(grad_bc_part.astype(jnp.bfloat16), "tensor")
-    grad_main = jnp.concatenate([grad_gate_z, grad_value, grad_step], 1).astype(jnp.bfloat16)
-    main_weight = back_in_weight[:, :main_cols]
-    bc_weight = back_in_weight[:, main_cols:]
-    bc_own = lax.dynamic_slice_in_dim(grad_bc, tensor_index * half_rows, half_rows, 0)
+    grad_gate_z = grad_gate_z.astype(jnp.bfloat16)
+    early = jnp.concatenate(
+        [contract_rows(normed_all, grad_gate_z), contract_rows(masked_cot, gnorm)], 1
+    ).astype(jnp.bfloat16)
+    early = lax.psum_scatter(early, "dp", scatter_dimension=0, tiled=True).astype(jnp.float32)
+    bc_own = lax.psum_scatter(
+        grad_bc_part.astype(jnp.bfloat16), "tensor", scatter_dimension=0, tiled=True
+    )
+    grad_main = jnp.concatenate([grad_value, grad_step], 1).astype(jnp.bfloat16)
+    late = jnp.concatenate(
+        [contract_rows(normed_all, grad_main), contract_rows(normed, bc_own)], 1
+    ).astype(jnp.bfloat16)
+    late = lax.psum_scatter(late, "dp", scatter_dimension=0, tiled=True).astype(jnp.float32)
+    side_cols = inner_local + heads_local
     grad_normed = lax.psum_scatter(
-        contract_cols(grad_main, main_weight).astype(jnp.bfloat16),
+        (
+            contract_cols(grad_gate_z, gate_weight)
+            + contract_cols(grad_main, side_weight[:, :side_cols])
+        ).astype(jnp.bfloat16),
         "tensor",
         scatter_dimension=0,
         tiled=True,
-    ).astype(jnp.float32) + contract_cols(bc_own, bc_weight)
-    weight_main = contract_rows(normed_all, grad_main)
-    weight_bc = contract_rows(normed_all, grad_bc)
+    ).astype(jnp.float32) + contract_cols(bc_own, side_weight[:, side_cols:])
     summed = (
-        lax.psum_scatter(weight_main[:, :inner_local], "dp", scatter_dimension=0, tiled=True),
-        lax.psum_scatter(
-            weight_main[:, inner_local : 2 * inner_local], "dp", scatter_dimension=0, tiled=True
-        ),
-        lax.psum_scatter(weight_bc, "dp", scatter_dimension=0, tiled=True),
-        lax.psum_scatter(weight_main[:, 2 * inner_local :], "dp", scatter_dimension=0, tiled=True),
-        lax.psum_scatter(grad_weight, "dp", scatter_dimension=1, tiled=True),
+        early[:, :inner_local],
+        late[:, :inner_local],
+        lax.psum(late[:, side_cols:], "tensor"),
+        late[:, inner_local:side_cols],
+        early[:, inner_local:].T,
     )
     grad_hat_in = grad_normed * norm_gain
     grad_in = in_rstd * (

time: 1070 us -> 716 us (0.67)
  waiting for transfers between devices: 361 us -> 173 us
  matrix products: 269 us -> 167 us
  blocking collectives: 93.4 us -> 62.5 us
  local copies, waits for them, and re-layouts: 122 us -> 103 us
  loops' own time: 12.7 us -> 0.85 us
  other arithmetic: 193 us -> 182 us
    reduce_scatter x4 -> x3, waiting for transfers between devices: 160 us -> 29 us  [the longest x1 29 us: body(): lax.psum_scatter((contract_cols(grad_gate_z, gate_weight) + contract_cols...]
    unnamed x16 -> x11, waiting for transfers between devices: 136 us -> 68.6 us
    dot_general x3, matrix products: 110 us -> 56 us  [scan_heads(): jnp.einsum('cijh,cjhp->cihp', score_weights, value_blocks, precision=PREC...]
    all_gather x2 -> x0, blocking collectives: 42 us -> none  [the longest x1 23.3 us: body(): lax.all_gather(proj_step, 'dp', axis=0, tiled=True)]
    dot_general x4, matrix products: 41.5 us -> 17.5 us  [scan_heads(): jnp.einsum('cjh,cjhp,cjn->chpn', tail_weight, value_blocks, key_blocks, p...]
    dot_general x4, matrix products: 37.6 us -> 13.9 us  [scan_heads(): jnp.einsum('cin,chpn->cihp', query_blocks, prior_state, precision=PRECISION)]
    another operation x3, other arithmetic: 19.6 us -> 0.17 us
    convert_element_type x0 -> x2, other arithmetic: none -> 16.7 us  [the longest x1 16.6 us: body(): grad_gate_z = grad_gate_z.astype(jnp.bfloat16)]
  transfers between devices with their start and end apart: 13 -> 9, of which waited for: 7 -> 5; matrix products, arithmetic and copies ran while one was open for 26% -> 29% of each run, Pallas kernels for 0% -> 0%
where the time goes in v1:
time: 716 us; the launch traced here: 705 us
  other arithmetic  182 us (25%)
  waiting for transfers between devices  173 us (24%)
  matrix products  167 us (23%)
  local copies, waits for them, and re-layouts  103 us (14%)
  blocking collectives  62.5 us (9%)
  between operations  16.4 us (2%)
    unnamed x11, waiting for transfers between devices  68.6 us
    dot_general x3, matrix products, scan_heads(): jnp.einsum('cijh,cjhp->cihp', score_weights, value_blocks, precision=PREC...  56 us
    unnamed x320, local copies, waits for them, and re-layouts  47.3 us
    all_gather x1, waiting for transfers between devices, body(): normed_all = lax.all_gather(normed, 'tensor', axis=0, tiled=True)  45.7 us
    psum x1, blocking collectives, body(): lax.psum((gain_part, g_conv_bc, g_conv_bc_bias, widen(g_conv_value, tenso...  41.2 us
    reduce_sum x4, other arithmetic, conv_seq(): kernel[kernel_size - 1 - offset] * moved  32.7 us
    all_gather x1, waiting for transfers between devices, body(): side_weight = lax.all_gather(side_pack, 'dp', axis=0, tiled=True)  29.9 us
    reduce_scatter x1, waiting for transfers between devices, body(): lax.psum_scatter((contract_cols(grad_gate_z, gate_weight) + contract_cols...  29 us
  transfers between devices with their start and end apart: 9, of which 5 were waited for; matrix products, arithmetic and copies ran while one was open for 29% of the time, Pallas kernels for 0%

profile of v1, /device:TPU:0, one launch (start us, length us, event | category | flops | bytes accessed | tf_op | source)
XLA Modules:
  0.0 705.2 jit_solution(16187825704945991356)
XLA Ops:
  24.0 29.9 %all-gather.7.cloned.1.call-done = bf16[768,1036]{1,0:T(8,128)(2,1)} async-done(((bf16[48,1036]{1,0:T(8,128)(2,1)}), bf16[768,1036]{1,0:T(8,128)(2,1)}) %all-gather.7.cloned.1.call-update) | async-done | bytes 1591312 | tf_op jit(solution)/shard_map/all_gather | solution.py:178
  53.9 45.7 %all-gather.5.cloned.1.call-done = bf16[2048,768]{1,0:T(8,128)(2,1)} async-done(((bf16[1024,768]{1,0:T(8,128)(2,1)}), bf16[2048,768]{1,0:T(8,128)(2,1)}) %all-gather.5.cloned.1.call-update) | async-done | bytes 3145744 | tf_op jit(solution)/shard_map/all_gather | solution.py:182
  99.6 6.2 fusion.178
  107.5 3.7 slice.259
  111.2 3.4 slice.257
  118.6 10.9 %fusion.170 = (f32[2048,768]{0,1:T(8,128)}, f32[2048,768]{0,1:T(8,128)S(1)}) fusion(f32[2048,1036]{0,1:T(8,128)S(1)} %fusion.178, f32[2048]{0:T(1024)} %copy-done.63, f32[2045,768]{0,1:T(8,128)S(1)} %slice.261, f32[768]{0:T(1024)S(1)} %copy-done.90, f32[2048]{0:T(1024)} %copy-done.64, f32[2046,768]{0,1:T(8,128)} %slice.259, f32[768]{0:T(1024)S(1)} %copy-done.88, ...), kind=kLoop, calls=%fused_computation.301 | loop fusion | flops 23592960 | bytes 37770240 | tf_op jit(solution)/shard_map/slice | solution.py:184
  134.1 3.7 fusion.40
  137.9 9.6 %while.52 = (s32[]{:T(128)}, f32[12,64,128]{2,1,0:T(8,128)S(1)}, bf16[8,12,64,128]{3,2,1,0:T(8,128)(2,1)S(1)}, f32[8,12]{1,0:T(8,128)S(1)}, f32[8,12,64,128]{3,2,1,0:T(8,128)}) while((s32[]{:T(128)}, f32[12,64,128]{2,1,0:T(8,128)S(1)}, bf16[8,12,64,128]{3,2,1,0:T(8,128)(2,1)S(1)}, f32[8,12]{1,0:T(8,128)S(1)}, ...), condition=%wide.region_4.5_spmd.clone.clone, body=%wide.region_3.4_spmd.clone.sunk.clone | while | flops 393219 | bytes 1769708 | solution.py:79
  148.7 15.6 %fusion.10 = f32[8,12,64,256]{3,2,1,0:T(8,128)S(1)} fusion(f32[8,256,12]{1,2,0:T(8,128)} %get-tuple-element.525, f32[8,256,256]{2,1,0:T(8,128)} %get-tuple-element.529, f32[8,256,12]{1,2,0:T(8,128)S(1)} %convolution_bitcast_fusion.2, f32[8,256,256]{2,1,0:T(8,128)S(1)} %fusion.99, pred[8,256,256]{2,1,0:T(8,128)(4,1)} %get-tuple-element.528, ...), kind=kOutput, calls=%fused_computation.25 | convolution fusion | flops 836763648 | bytes 17498112 | tf_op jit(solution)/shard_map/jvp(cijh,cjhp->cihp)/dot_general | solution.py:64
  167.5 4.4 copy.215
  171.9 5.7 copy.285
  177.5 14.7 %multiply_reduce_fusion.10 = (f32[2048]{0:T(1024)S(1)}, f32[2048,768]{0,1:T(8,128)}, f32[2048,768]{0,1:T(8,128)}) fusion(f32[2048,768]{0,1:T(8,128)} %bitcast.290, f32[2048,768]{0,1:T(8,128)} %copy-done.3, f32[768]{0:T(1024)S(1)} %copy-done.86, bf16[2048,768]{1,0:T(8,128)(2,1)} %all-gather.5.cloned.1.call-done, ...), kind=kOutput, calls=%fused_computation.76 | convolution fusion | flops 2430072832 | bytes 29502464 | tf_op jit(solution)/shard_map/dot_general | solution.py:187
  192.3 5.0 psum.84
  197.3 11.0 %multiply_reduce_fusion.2 = (f32[768]{0:T(1024)}, f32[2048]{0:T(1024)S(1)}, f32[2048,768]{0,1:T(8,128)}) fusion(f32[2048,768]{0,1:T(8,128)} %get-tuple-element.494, f32[2048]{0:T(1024)S(1)} %get-tuple-element.538, f32[768]{0:T(1024)S(1)} %copy-done.108, bf16[768,1536]{1,0:T(8,128)(2,1)} %all-gather.9.cloned.1.call-done, ...), kind=kOutput, calls=%fused_computation.60 | convolution fusion | flops 2426926336 | bytes 16934912 | tf_op jit(solution)/shard_map/dot_general | solution.py:219
  208.3 5.0 psum.85
  213.3 16.6 %multiply_convert_fusion = (bf16[2048,768]{0,1:T(8,128)(2,1)}, f32[2048,768]{0,1:T(8,128)}) fusion(f32[2048,768]{0,1:T(8,128)} %get-tuple-element.554, f32[2048]{0:T(1024)S(1)} %broadcast_multiply_fusion.6, f32[2048,768]{0,1:T(8,128)} %get-tuple-element.494, f32[2048]{0:T(1024)S(1)} %get-tuple-element.537, f32[2048,768]{0,1:T(8,128)} %get-tuple-element.555, ...), kind=kLoop, calls=%fused_computation.72 | loop fusion | flops 29884416 | bytes 40925184 | tf_op jit(solution)/shard_map/convert_element_type | solution.py:242
  243.1 8.6 %copy.287 = f32[96,8,8,256]{3,2,1,0:T(8,128)} copy(f32[96,8,8,256]{3,1,2,0:T(8,128)} %bitcast.278) | data formatting | bytes 12582912
  251.8 9.4 %multiply_reduce_fusion.3 = (f32[768]{0:T(1024)}, f32[2048,768]{0,1:T(8,128)S(1)}) fusion(f32[2048,768]{0,1:T(8,128)} %get-tuple-element.251, f32[2048]{0:T(1024)S(1)} %copy-done.45, f32[2045,768]{0,1:T(8,128)S(1)} %bitcast.254, f32[768]{0:T(1024)S(1)} %copy-done.73, f32[2048]{0:T(1024)S(1)} %copy-done.50, f32[2046,768]{0,1:T(8,128)S(1)} %bitcast.255, ...), kind=kLoop, calls=%fused_computation.61 | loop fusion | flops 26737920 | bytes 37773312 | tf_op jit(solution)/shard_map/transpose(jvp(jvp()))/checkpoint/reduce_sum | solution.py:113
  268.2 3.7 fusion.50
  271.8 19.9 %while.53 = (s32[]{:T(128)}, f32[12,64,128]{2,1,0:T(8,128)S(1)}, f32[8,12,64,128]{3,2,1,0:T(8,128)}, f32[8,12,1,1]{1,3,2,0:T(1,128)}, f32[8,12]{1,0:T(8,128)S(1)}, /*index=5*/f32[8,12,64,128]{3,2,1,0:T(8,128)}) while((s32[]{:T(128)}, f32[12,64,128]{2,1,0:T(8,128)S(1)}, f32[8,12,64,128]{3,2,1,0:T(8,128)}, ...), condition=%wide.region_11.12_spmd.clone.clone, body=%wide.region_10.11_spmd.clone.sunk.clone | while | flops 393219 | bytes 1966888 | solution.py:79
  291.7 6.6 fusion.47
  304.7 22.0 %while.54 = (s32[]{:T(128)}, f32[12,64,128]{2,1,0:T(8,128)S(1)}, f32[8,12]{1,0:T(8,128)S(1)}, bf16[8,12,64,128]{3,2,1,0:T(8,128)(2,1)}, f32[8,12,64,128]{3,2,1,0...) while((s32[]{:T(128)}, f32[12,64,128]{2,1,0:T(8,128)S(1)}, ...), condition=%wide.region_14.15_spmd.clone.clone, body=%wide.region_12.14_spmd.clone.sunk.clone | while | flops 589816 | bytes 2163100 | solution.py:79
  326.8 6.4 fusion.94
  333.2 3.7 fusion.179
  339.6 9.1 %multiply_reduce_fusion.1 = f32[8,256,12]{1,0,2:T(8,128)S(1)} fusion(f32[8,256,12,64]{1,0,3,2:T(8,128)} %bitcast.276, f32[8,256,12,64]{1,3,2,0:T(8,128)} %fusion.179), kind=kLoop, calls=%fused_computation.59 | loop fusion | flops 3121152 | bytes 12681216
  351.3 28.1 %fusion.18 = (f32[8,256,12]{1,2,0:T(8,128)}, f32[8,256,12]{1,2,0:T(8,128)}, f32[8,256,12]{1,2,0:T(8,128)}, bf16[8,256,256]{2,1,0:T(8,128)(2,1)}) fusion(f32[8,256,12]{1,2,0:T(8,128)} %get-tuple-element.524, f32[8,256,256]{2,1,0:T(8,128)} %get-tuple-element.527, f32[8,256,12]{1,2,0:T(8,128)S(1)} %copy-done.30, f32[8,256,256]{2,1,0:T(8,128)} %fusion.180, ...), kind=kOutput, calls=%fused_computation.33 | convolution fusion | flops 899080192 | bytes 18841600 | tf_op jit(solution)/shard_map/transpose(jvp(jvp()))/checkpoint/cijh,cjhp->cihp/dot_general | solution.py:64
  379.5 12.2 %bitcast_add_fusion.3 = f32[8,256,12,64]{1,3,2,0:T(8,128)} fusion(f32[8,256,12,64]{1,3,2,0:T(8,128)S(1)} %bitcast.283, f32[8,256,12]{1,2,0:T(8,128)S(1)} %copy-done.33, f32[8,256,12]{1,2,0:T(8,128)} %get-tuple-element.524, f32[8,256,256]{2,1,0:T(8,128)} %get-tuple-element.527, f32[8,256,12]{1,2,0:T(8,128)S(1)} %copy-done.30, f32[8,256,256]{2,1,0:T(8,128)} %fusion.180, ...), kind=kOutput, calls=%fused_computation.54 | convolution fusion | flops 839909376 | bytes 23887872 | tf_op jit(solution)/shard_map/transpose(jvp(jvp()))/checkpoint/cijh,cjhp->cihp/dot_general | solution.py:64
  391.9 6.6 fusion.90
  402.8 4.7 copy.275
  416.1 7.2 %copy.228 = f32[8,256,12,64]{1,0,3,2:T(8,128)S(1)} copy(f32[8,256,12,64]{1,3,2,0:T(8,128)} %bitcast_add_fusion.3) | data formatting | bytes 12582912 | tf_op jit(solution)/shard_map/transpose(jvp(jvp()))/checkpoint/cijh,cjhp->cihp/add_any | solution.py:64
  423.3 5.7 copy.291
  437.8 15.3 %multiply_reduce_fusion.7 = (f32[768]{0:T(1024)S(1)}, f32[2048,768]{0,1:T(8,128)}, f32[2048,768]{0,1:T(8,128)}) fusion(f32[2045,768]{0,1:T(8,128)} %bitcast.249, f32[2048]{0:T(1024)S(1)} %copy-done.45, f32[2048,768]{0,1:T(8,128)} %copy-done.2, f32[2048,768]{0,1:T(8,128)} %bitcast.289, f32[2048,768]{0,1:T(8,128)} %get-tuple-element.251, f32[768]{0:T(1024)S(1)} %mul.991), kind=kLoop, calls=%fused_computation.65 | loop fusion | flops 22019328 | bytes 37753856 | tf_op jit(solution)/shard_map/transpose(jvp(jvp()))/checkpoint/reduce_sum | solution.py:35
  454.3 13.5 %multiply_reduce_fusion.6 = (f32[768]{0:T(1024)S(1)}, f32[2048,768]{0,1:T(8,128)}, f32[768]{0:T(1024)S(1)}, f32[2048,768]{0,1:T(8,128)}) fusion(f32[2046,768]{0,1:T(8,128)} %bitcast.250, f32[2048,768]{0,1:T(8,128)} %get-tuple-element.486, f32[2048]{0:T(1024)S(1)} %copy-done.51, f32[2047,768]{0,1:T(8,128)} %bitcast.251, f32[2048]{0:T(1024)S(1)} %copy-done.48), kind=kLoop, calls=%fused_computation.64 | loop fusion | flops 9435648 | bytes 31470592 | tf_op jit(solution)/shard_map/transpose(jvp(jvp()))/checkpoint/reduce_sum | solution.py:35
  467.8 4.6 slice_multiply_fusion.2
  472.7 7.3 %slice_multiply_fusion.1 = f32[2046,768]{0,1:T(8,128)} fusion(f32[2048,768]{0,1:T(8,128)} %get-tuple-element.488, f32[768]{0:T(1024)S(1)} %copy-done.72), kind=kLoop, calls=%fused_computation.52 | loop fusion | flops 1571328 | bytes 12573696 | tf_op jit(solution)/shard_map/transpose(jvp(jvp()))/checkpoint/mul | solution.py:35
  480.1 5.1 slice_multiply_fusion
  487.3 8.2 %fusion.162 = (f32[768]{0:T(1024)S(1)}, f32[768]{0:T(1024)S(1)}, bf16[2048,768]{0,1:T(8,128)(2,1)S(1)}) fusion(f32[2048,768]{0,1:T(8,128)} %get-tuple-element.486, f32[2048,768]{0,1:T(8,128)S(1)} %bitcast.258, f32[768]{0:T(1024)S(1)} %copy-done.68, f32[2047,768]{0,1:T(8,128)} %slice_multiply_fusion, f32[2046,768]{0,1:T(8,128)} %slice_multiply_fusion.1, ...), kind=kLoop, calls=%fused_computation.297 | loop fusion | flops 12581376 | bytes 34593792 | tf_op jit(solution)/shard_map/transpose(jvp(jvp()))/checkpoint/reduce_sum | solution.py:29
  497.3 5.8 fusion.89
  507.5 6.0 fusion.86
  513.5 4.2 add_convert_fusion
  517.8 7.7 %convolution_convert_fusion = bf16[2048,768]{1,0:T(8,128)(2,1)} fusion(bf16[768,1536]{1,0:T(8,128)(2,1)} %all-gather.9.cloned.1.call-done, f32[2048,768]{0,1:T(8,128)} %get-tuple-element.494, f32[768]{0:T(1024)S(1)} %copy-done.110, f32[2048]{0:T(1024)S(1)} %copy-done.78), kind=kOutput, calls=%fused_computation.104 | convolution fusion | flops 2422210560 | bytes 10628096 | tf_op jit(solution)/shard_map/dot_general | solution.py:124
  527.8 7.8 %reduce-scatter.16.cloned.1.call-done = bf16[48,1536]{1,0:T(8,128)(2,1)} async-done(((bf16[768,1536]{1,0:T(8,128)(2,1)}), bf16[48,1536]{1,0:T(8,128)(2,1)}) %reduce-scatter.16.cloned.1.call-update) | async-done | bytes 147472
  538.5 60.1 %reduce-scatter.18.cloned.1.call-done = bf16[48,1036]{1,0:T(8,128)(2,1)} async-done(((bf16[768,1036]{1,0:T(8,128)(2,1)}), bf16[48,1036]{1,0:T(8,128)(2,1)}) %reduce-scatter.18.cloned.1.call-update) | async-done | bytes 99472
  601.0 11.3 %psum.87 = f32[48,256]{0,1:T(8,128)S(1)} all-reduce(f32[48,256]{0,1:T(8,128)S(1)} %copy.385), channel_id=1, replica_groups=mesh['dp'=16,'tensor'=2] {'tensor'}, use_global_device_ids=true, to_apply=%region_28.29 | all-reduce | flops 12288 | bytes 98304 | tf_op jit(solution)/shard_map/psum | solution.py:268
  614.9 29.0 %reduce-scatter.12.cloned.1.call-done = bf16[1024,768]{1,0:T(8,128)(2,1)} async-done(((bf16[2048,768]{1,0:T(8,128)(2,1)}), bf16[1024,768]{1,0:T(8,128)(2,1)}) %reduce-scatter.12.cloned.1.call-update) | async-done | bytes 1572880 | tf_op jit(solution)/shard_map/reduce_scatter | solution.py:256
  643.9 4.8 fusion.65
  648.7 41.2 %all-reduce.35 = (f32[768]{0:T(1024)}, f32[4,1536]{1,0:T(4,128)S(1)}, f32[1536]{0:T(1024)S(1)}, f32[4,256]{1,0:T(4,128)}, f32[256]{0:T(256)}, /*index=5*/f32[24]...) all-reduce(f32[768]{0:T(1024)S(1)} %get-tuple-element.416, ...), channel_id=1, replica_groups=mesh['dp'=16,'tensor'=2] {'dp','tensor'}, use_global_device_ids=true, to_apply=%region_25.26 | all-reduce | flops 11336 | bytes 90688 | tf_op jit(solution)/shard_map/psum | solution.py:278
  693.6 4.6 fusion.64
  (568 shorter events, 157.5 us)
Async XLA Ops:
  7.2 46.7 %all-gather.7.cloned.1.call-start = ((), (), s32[]{:S(2)}) async-start(), calls=%async_computation.6 | async-start | bytes 1880064 | tf_op jit(solution)/shard_map/all_gather | solution.py:178
  9.7 89.9 %all-gather.5.cloned.1.call-start = ((), (), s32[]{:S(2)}) async-start(), calls=%async_computation.5 | async-start | bytes 4718592 | tf_op jit(solution)/shard_map/all_gather | solution.py:182
  14.6 162.9 %all-gather.9.cloned.1.call-start = ((), (), s32[]{:S(2)}) async-start(), calls=%async_computation.7 | async-start | bytes 2506752 | tf_op jit(solution)/shard_map/all_gather | solution.py:179
  15.3 181.9 %all-gather.11.cloned.1.call-start = ((), (), s32[]{:S(2)}) async-start(), calls=%async_computation.9 | async-start | bytes 4718592 | tf_op jit(solution)/shard_map/all_gather | solution.py:218
  15.9 487.1 %reduce-scatter.14.cloned.1.call-start = ((), (), s32[]{:S(2)}) async-start(), calls=%async_computation.11 | async-start | bytes 1572864 | tf_op jit(solution)/shard_map/reduce_scatter | solution.py:247
  17.8 88.0 %copy-start.8 = (bf16[8,12,64,128]{3,2,1,0:T(8,128)(2,1)}, bf16[8,12,64,128]{3,2,1,0:T(8,128)(2,1)S(1)}, u32[]{:S(2)}) copy-start(bf16[8,12,64,128]{3,2,1,0:T(8,128)(2,1)S(1)} %fusion.171) | copy-start | bytes 4718596
  23.9 92.0 %copy-start.63 = (f32[2048]{0:T(1024)}, f32[2048]{0:T(1024)S(1)}, u32[]{:S(2)}) copy-start(f32[2048]{0:T(1024)S(1)} %get-tuple-element.544) | copy-start | bytes 24580
  23.9 92.0 %copy-start.64 = (f32[2048]{0:T(1024)}, f32[2048]{0:T(1024)S(1)}, u32[]{:S(2)}) copy-start(f32[2048]{0:T(1024)S(1)} %get-tuple-element.545) | copy-start | bytes 24580
  105.8 12.7 %copy-start = (f32[2048,1036]{0,1:T(8,128)}, f32[2048,1036]{0,1:T(8,128)S(1)}, u32[]{:S(2)}) copy-start(f32[2048,1036]{0,1:T(8,128)S(1)} %fusion.178) | copy-start | bytes 25460740
  177.5 19.8 %copy-start.108 = (f32[768]{0:T(1024)S(1)}, f32[768]{0:T(1024)}, u32[]{:S(2)}) copy-start(f32[768]{0:T(1024)} %param.41) | copy-start | bytes 9220
  177.5 19.8 %copy-start.116 = (bf16[2048]{0:T(1024)(128)(2,1)S(1)}, bf16[2048]{0:T(1024)(128)(2,1)}, u32[]{:S(2)}) copy-start(bf16[2048]{0:T(1024)(128)(2,1)} %fusion.152) | copy-start | bytes 12292
  197.2 16.0 %copy-start.77 = (f32[2048]{0:T(1024)}, f32[2048]{0:T(1024)S(1)}, u32[]{:S(2)}) copy-start(f32[2048]{0:T(1024)S(1)} %get-tuple-element.538) | copy-start | bytes 24580
  213.3 17.6 %copy-start.41 = (pred[256,256]{1,0:T(8,128)(4,1)S(1)}, pred[256,256]{1,0:T(8,128)(4,1)}, u32[]{:S(2)}) copy-start(pred[256,256]{1,0:T(8,128)(4,1)} %copy-done.40) | copy-start | bytes 196612
  213.3 19.5 %copy-start.130 = (f32[12]{0:T(128)S(1)}, f32[12]{0:T(128)}, u32[]{:S(2)}) copy-start(f32[12]{0:T(128)} %param.39) | copy-start | bytes 148
  213.3 19.5 %copy-start.92 = (f32[4,256]{1,0:T(4,128)S(1)}, f32[4,256]{1,0:T(4,128)}, u32[]{:S(2)}) copy-start(f32[4,256]{1,0:T(4,128)} %param.36) | copy-start | bytes 12292
  213.3 20.8 %copy-start.66 = (f32[4,768]{1,0:T(4,128)S(1)}, f32[4,768]{1,0:T(4,128)}, u32[]{:S(2)}) copy-start(f32[4,768]{1,0:T(4,128)} %param.34) | copy-start | bytes 36868
  213.3 21.4 %copy-start.36 = (f32[2048,12]{0,1:T(8,128)S(1)}, f32[2048,12]{0,1:T(8,128)}, u32[]{:S(2)}) copy-start(f32[2048,12]{0,1:T(8,128)} %get-tuple-element.256) | copy-start | bytes 294916
  213.3 21.4 %copy-start.104 = (f32[12]{0:T(128)S(1)}, f32[12]{0:T(128)}, u32[]{:S(2)}) copy-start(f32[12]{0:T(128)} %param.38) | copy-start | bytes 148
  304.7 22.1 %copy-start.32 = (f32[8,256,12]{1,2,0:T(8,128)S(1)}, f32[8,256,12]{1,2,0:T(8,128)}, u32[]{:S(2)}) copy-start(f32[8,256,12]{1,2,0:T(8,128)} %copy-done.31) | copy-start | bytes 294916
  349.5 29.9 %slice-start.6 = ((s8[6291456]{0:T(1024)(128)(4,1)}), s8[4194304]{0:T(1024)(128)(4,1)S(1)}, s32[]{:S(2)}) async-start(s8[6291456]{0:T(1024)(128)(4,1)} %bitcast.271), calls=%async_computation.20 | async-start | bytes 8388608
  349.5 29.9 %slice-start.8 = ((s8[6291456]{0:T(1024)(128)(4,1)}), s8[4194304]{0:T(1024)(128)(4,1)S(1)}, s32[]{:S(2)}) async-start(s8[6291456]{0:T(1024)(128)(4,1)} %bitcast.282), calls=%async_computation.22 | async-start | bytes 8388608
  351.3 28.2 %slice-start.7 = ((s8[6291456]{0:T(1024)(128)(4,1)}), s8[2097152]{0:T(1024)(128)(4,1)S(1)}, s32[]{:S(2)}) async-start(s8[6291456]{0:T(1024)(128)(4,1)} %bitcast.271), calls=%async_computation.21 | async-start | bytes 4194304
  351.3 28.2 %slice-start.9 = ((s8[6291456]{0:T(1024)(128)(4,1)}), s8[2097152]{0:T(1024)(128)(4,1)S(1)}, s32[]{:S(2)}) async-start(s8[6291456]{0:T(1024)(128)(4,1)} %bitcast.282), calls=%async_computation.23 | async-start | bytes 4194304
  351.3 28.2 %copy-start.33 = (f32[8,256,12]{1,2,0:T(8,128)S(1)}, f32[8,256,12]{1,2,0:T(8,128)}, u32[]{:S(2)}) copy-start(f32[8,256,12]{1,2,0:T(8,128)} %copy-done.31) | copy-start | bytes 294916
  437.6 98.0 %reduce-scatter.16.cloned.1.call-start = ((), (), s32[]{:S(2)}) async-start(), calls=%async_computation.12 | async-start | bytes 2506752
  437.6 15.4 %copy-start.94 = (f32[8,12]{1,0:T(8,128)S(1)}, f32[8,12]{1,0:T(8,128)}, u32[]{:S(2)}) copy-start(f32[8,12]{1,0:T(8,128)} %copy-done.93) | copy-start | bytes 1156
  437.7 15.4 %copy-start.107 = (f32[8]{0:T(128)S(1)}, f32[8]{0:T(128)}, u32[]{:S(2)}) copy-start(f32[8]{0:T(128)} %convert_reduce_fusion.1) | copy-start | bytes 100
  437.7 15.6 %copy-start.39 = (f32[8,256,12]{1,0,2:T(8,128)S(1)}, f32[8,256,12]{1,0,2:T(8,128)}, u32[]{:S(2)}) copy-start(f32[8,256,12]{1,0,2:T(8,128)} %copy-done.38) | copy-start | bytes 294916
  437.7 15.6 %copy-start.43 = (f32[8,256,12]{1,2,0:T(8,128)S(1)}, f32[8,256,12]{1,2,0:T(8,128)}, u32[]{:S(2)}) copy-start(f32[8,256,12]{1,2,0:T(8,128)} %multiply_reduce_fusion.8) | copy-start | bytes 294916
  437.7 15.6 %copy-start.54 = (f32[8,256,12]{1,2,0:T(8,128)S(1)}, f32[8,256,12]{1,2,0:T(8,128)}, u32[]{:S(2)}) copy-start(f32[8,256,12]{1,2,0:T(8,128)} %get-tuple-element.408) | copy-start | bytes 294916
  437.7 15.6 %copy-start.55 = (f32[8,256,12]{1,2,0:T(8,128)S(1)}, f32[8,256,12]{1,2,0:T(8,128)}, u32[]{:S(2)}) copy-start(f32[8,256,12]{1,2,0:T(8,128)} %get-tuple-element.409) | copy-start | bytes 294916
  437.7 15.6 %copy-start.56 = (f32[8,256,12]{1,2,0:T(8,128)S(1)}, f32[8,256,12]{1,2,0:T(8,128)}, u32[]{:S(2)}) copy-start(f32[8,256,12]{1,2,0:T(8,128)} %get-tuple-element.410) | copy-start | bytes 294916
  437.7 15.6 %copy-start.62 = (f32[8,256]{1,0:T(8,128)S(1)}, f32[8,256]{1,0:T(8,128)}, u32[]{:S(2)}) copy-start(f32[8,256]{1,0:T(8,128)} %copy-done.61) | copy-start | bytes 24580
  437.7 15.6 %copy-start.121 = (f32[12]{0:T(128)S(1)}, f32[12]{0:T(128)}, u32[]{:S(2)}) copy-start(f32[12]{0:T(128)} %copy-done.120) | copy-start | bytes 148
  437.7 16.2 %copy-start.37 = (f32[2048,12]{0,1:T(8,128)S(1)}, f32[2048,12]{0,1:T(8,128)}, u32[]{:S(2)}) copy-start(f32[2048,12]{0,1:T(8,128)} %get-tuple-element.256) | copy-start | bytes 294916
  437.7 16.2 %copy-start.105 = (f32[12]{0:T(128)S(1)}, f32[12]{0:T(128)}, u32[]{:S(2)}) copy-start(f32[12]{0:T(128)} %param.38) | copy-start | bytes 148
  453.9 13.9 %slice-start.10 = ((s8[6291456]{0:T(1024)(128)(4,1)}), s8[4194304]{0:T(1024)(128)(4,1)S(1)}, s32[]{:S(2)}) async-start(s8[6291456]{0:T(1024)(128)(4,1)} %bitcast.287), calls=%async_computation.24 | async-start | bytes 8388608
  454.3 13.5 %slice-start.11 = ((s8[6291456]{0:T(1024)(128)(4,1)}), s8[2097152]{0:T(1024)(128)(4,1)S(1)}, s32[]{:S(2)}) async-start(s8[6291456]{0:T(1024)(128)(4,1)} %bitcast.287), calls=%async_computation.25 | async-start | bytes 4194304
  454.3 13.5 %copy-start.74 = (f32[768]{0:T(1024)S(1)}, f32[768]{0:T(1024)}, u32[]{:S(2)}) copy-start(f32[768]{0:T(1024)} %get-tuple-element.420) | copy-start | bytes 9220
  472.4 126.2 %reduce-scatter.18.cloned.1.call-start = ((), (), s32[]{:S(2)}) async-start(), calls=%async_computation.13 | async-start | bytes 1880064
  507.1 136.7 %reduce-scatter.12.cloned.1.call-start = ((), (), s32[]{:S(2)}) async-start(), calls=%async_computation.10 | async-start | bytes 4718592 | tf_op jit(solution)/shard_map/reduce_scatter | solution.py:256
  517.8 175.8 %reduce-scatter.10.cloned.1.call-start = ((), (), s32[]{:S(2)}) async-start(), calls=%async_computation.8 | async-start | bytes 4718592 | tf_op jit(solution)/shard_map/reduce_scatter | solution.py:209
  526.3 88.6 %copy-start.81 = (f32[2048]{0:T(1024)}, f32[2048]{0:T(1024)S(1)}, u32[]{:S(2)}) copy-start(f32[2048]{0:T(1024)S(1)} %fusion.143) | copy-start | bytes 24580
  527.7 116.1 %copy-start.13 = (bf16[1024,768]{1,0:T(8,128)(2,1)S(1)}, bf16[1024,768]{1,0:T(8,128)(2,1)}, u32[]{:S(2)}) copy-start(bf16[1024,768]{1,0:T(8,128)(2,1)} %param.24) | copy-start | bytes 4718596
  527.7 116.1 %copy-start.76 = (f32[1024]{0:T(1024)S(1)}, f32[1024]{0:T(1024)}, u32[]{:S(2)}) copy-start(f32[1024]{0:T(1024)} %copy-done.75) | copy-start | bytes 12292
  527.7 116.1 %copy-start.84 = (f32[768]{0:T(1024)S(1)}, f32[768]{0:T(1024)}, u32[]{:S(2)}) copy-start(f32[768]{0:T(1024)} %param.28) | copy-start | bytes 9220
  614.9 33.8 %copy-start.111 = (f32[256]{0:T(256)S(1)}, f32[256]{0:T(256)}, u32[]{:S(2)}) copy-start(f32[256]{0:T(256)} %get-tuple-element.418) | copy-start | bytes 3076
  643.9 49.7 %dynamic-slice-start = ((f32[2048]{0:T(1024)}, s32[]{:T(128)}), f32[1024]{0:T(1024)S(1)}, s32[]{:S(2)}) async-start(f32[2048]{0:T(1024)} %copy-done.81, s32[]{:T(128)} %select_n.47), calls=%async_computation.28 | async-start | bytes 8704 | tf_op jit(solution)/shard_map/dynamic_slice | solution.py:215
  (110 other events, 538.8 us)
Sparse Core Ops, SparseCore 0:
  10.8 43.0 all-gather.6
  56.0 43.5 all-gather.4
  102.5 42.2 all-gather.8
  146.1 43.6 all-gather.10
  437.7 20.5 reduce-scatter.13
  472.5 63.0 reduce-scatter.15
  539.4 59.2 reduce-scatter.17
  600.9 42.9 reduce-scatter.11
  646.2 44.7 reduce-scatter.9

commit v2 on v1

--- a/solution.py
+++ b/solution.py
@@ -3,13 +3,14 @@
 import jax
 import jax.numpy as jnp
 from jax import lax
+from jax.experimental import pallas as pl
+from jax.experimental.pallas import tpu as pltpu
 from jax.sharding import PartitionSpec as P
 
 BLOCK = 256
 
 
 EPSILON = 1e-05
-PRECISION = lax.Precision.DEFAULT
 SUM_PRECISION = lax.Precision.HIGHEST
 
 
@@ -39,53 +40,7 @@
     return result
 
 
-def scan_heads(values, keys_b, query_c, step_size, decay_rate, segment):
-    row_count, head_count, head_dim = values.shape
-    state_size = keys_b.shape[1]
-    blocks = row_count // BLOCK
-    value_blocks = values.reshape(blocks, BLOCK, head_count, head_dim)
-    step_blocks = step_size.reshape(blocks, BLOCK, head_count)
-    key_blocks = keys_b.reshape(blocks, BLOCK, state_size)
-    query_blocks = query_c.reshape(blocks, BLOCK, state_size)
-    segment_blocks = segment.reshape(blocks, BLOCK)
-    lower_mask = jnp.arange(BLOCK)[:, None] >= jnp.arange(BLOCK)[None, :]
-    rates = step_blocks * decay_rate
-    cum_rates = jnp.einsum(
-        "ij,cjh->cih", lower_mask.astype(jnp.float32), rates, precision=SUM_PRECISION
-    )
-    same_segment = lower_mask[None] & (segment_blocks[:, :, None] == segment_blocks[:, None, :])
-    rate_gaps = cum_rates[:, :, None, :] - cum_rates[:, None, :, :]
-    decays = (
-        jnp.exp(jnp.where(same_segment[..., None], rate_gaps, 0.0))
-        * same_segment.astype(jnp.float32)[..., None]
-    )
-    scores = jnp.einsum("cin,cjn->cij", query_blocks, key_blocks, precision=PRECISION)
-    score_weights = scores[..., None] * decays * step_blocks[:, None, :, :]
-    inside = jnp.einsum("cijh,cjhp->cihp", score_weights, value_blocks, precision=PRECISION)
-    last_rate = cum_rates[:, -1, :]
-    tail_mask = (segment_blocks == segment_blocks[:, -1:]).astype(jnp.float32)
-    tail_weight = jnp.exp(last_rate[:, None, :] - cum_rates) * tail_mask[..., None] * step_blocks
-    states = jnp.einsum(
-        "cjh,cjhp,cjn->chpn", tail_weight, value_blocks, key_blocks, precision=PRECISION
-    )
-    prev_last = jnp.concatenate([jnp.full((1,), -2, jnp.int32), segment_blocks[:-1, -1]])
-    keep_flag = (segment_blocks[:, -1] == prev_last).astype(jnp.float32)
-    carry_gain = jnp.exp(last_rate) * keep_flag[:, None]
-
-    def advance(carry_state, block_item):
-        gain_now, fresh_state = block_item
-        return (gain_now[:, None, None] * carry_state + fresh_state, carry_state)
-
-    ended, prior_state = lax.scan(
-        advance, jnp.zeros((head_count, head_dim, state_size), jnp.float32), (carry_gain, states)
-    )
-    head_same = (segment_blocks == prev_last[:, None]).astype(jnp.float32)
-    carried = jnp.einsum("cin,chpn->cihp", query_blocks, prior_state, precision=PRECISION)
-    carried = carried * (jnp.exp(cum_rates) * head_same[..., None])[..., None]
-    return (inside + carried).reshape(row_count, head_count, head_dim)
-
-
-def mixer(
+def prepare(
     value_proj,
     bc_proj,
     step_raw,
@@ -95,23 +50,241 @@
     conv_bc_bias,
     step_bias,
     decay_log,
-    skip_gain,
     segment,
 ):
-    conv_out = jax.nn.silu(conv_seq(value_proj, conv_value, conv_value_bias, segment))
+    values = jax.nn.silu(conv_seq(value_proj, conv_value, conv_value_bias, segment))
     bc_conv = jax.nn.silu(conv_seq(bc_proj, conv_bc, conv_bc_bias, segment))
     state_size = bc_proj.shape[1] // 2
     step_size = jax.nn.softplus(step_raw + step_bias)
-    decay_rate = -jnp.exp(decay_log)
-    row_count = value_proj.shape[0]
-    head_count = step_size.shape[1]
-    head_dim = value_proj.shape[1] // head_count
-    values = conv_out.reshape(row_count, head_count, head_dim)
-    mixed_out = scan_heads(
-        values, bc_conv[:, :state_size], bc_conv[:, state_size:], step_size, decay_rate, segment
-    )
-    mixed_out = mixed_out + skip_gain[None, :, None] * values
-    return mixed_out.reshape(row_count, head_count * head_dim)
+    row_count, head_count = step_size.shape
+    blocks = row_count // BLOCK
+    rates = (step_size * -jnp.exp(decay_log)).reshape(blocks, BLOCK, head_count)
+    segment_blocks = segment.reshape(blocks, BLOCK)
+    lower_mask = jnp.arange(BLOCK)[:, None] >= jnp.arange(BLOCK)[None, :]
+    cum_rates = jnp.einsum(
+        "ij,cjh->cih", lower_mask.astype(jnp.float32), rates, precision=SUM_PRECISION
+    )
+    last_rate = cum_rates[:, -1, :]
+    prev_last = jnp.concatenate([jnp.full((1,), -2, jnp.int32), segment_blocks[:-1, -1]])
+    tail_mask = (segment_blocks == segment_blocks[:, -1:]).astype(jnp.float32)
+    head_same = (segment_blocks == prev_last[:, None]).astype(jnp.float32)
+    keep_flag = (segment_blocks[:, -1] == prev_last).astype(jnp.float32)
+    tail = jnp.exp(last_rate[:, None, :] - cum_rates) * tail_mask[..., None]
+    edge = jnp.exp(cum_rates) * head_same[..., None]
+    gain = jnp.exp(last_rate) * keep_flag[:, None]
+    flat = (row_count, head_count)
+    return (
+        values,
+        bc_conv[:, :state_size],
+        bc_conv[:, state_size:],
+        step_size,
+        cum_rates.reshape(flat),
+        edge.reshape(flat),
+        tail.reshape(flat),
+        jnp.repeat(gain, values.shape[1] // head_count, axis=1)[:, None, :],
+    )
+
+
+def block_mask(seg_col, seg_row):
+    shape = (BLOCK, BLOCK)
+    lower = lax.broadcasted_iota(jnp.int32, shape, 0) >= lax.broadcasted_iota(jnp.int32, shape, 1)
+    return lower & (seg_col[...] == seg_row[...])
+
+
+def pick(ref, pair, low_lane):
+    return jnp.where(low_lane, ref[:, 2 * pair : 2 * pair + 1], ref[:, 2 * pair + 1 : 2 * pair + 2])
+
+
+def scan_forward_kernel(
+    v, b, c, step, cum, edge, tail, gain, cum_row, seg_col, seg_row, skip, y, prior, state
+):
+    @pl.when(pl.program_id(0) == 0)
+    def _():
+        state[...] = jnp.zeros_like(state)
+
+    prior[...] = state[...]
+    keys = b[...].astype(jnp.bfloat16)
+    queries = c[...].astype(jnp.bfloat16)
+    scores = contract_cols(queries, keys)
+    mask = block_mask(seg_col, seg_row)
+    low_lane = lax.broadcasted_iota(jnp.int32, (BLOCK, 128), 1) < 64
+    for pair in range(v.shape[1] // 128):
+        cols = slice(128 * pair, 128 * pair + 128)
+        values = v[:, cols]
+        scaled = values * pick(step, pair, low_lane)
+        scaled_low = scaled.astype(jnp.bfloat16)
+        inside = []
+        for head in (2 * pair, 2 * pair + 1):
+            gap = cum[:, head : head + 1] - cum_row[head : head + 1, :]
+            weight = scores * jnp.exp(jnp.where(mask, gap, -1e30))
+            inside.append(dot_rows(weight.astype(jnp.bfloat16), scaled_low))
+        before = state[:, cols]
+        carried = dot_rows(queries, before.astype(jnp.bfloat16)) * pick(edge, pair, low_lane)
+        y[:, cols] = jnp.where(low_lane, inside[0], inside[1]) + carried + skip[:, cols] * values
+        fresh = (scaled * pick(tail, pair, low_lane)).astype(jnp.bfloat16)
+        state[:, cols] = gain[0, :, cols] * before + contract_rows(keys, fresh)
+
+
+def scan_backward_kernel(
+    v,
+    b,
+    c,
+    step,
+    cum,
+    edge,
+    tail,
+    gain,
+    cum_row,
+    seg_col,
+    seg_row,
+    skip,
+    dy,
+    prior,
+    dv,
+    db,
+    dc,
+    dstep,
+    dcum,
+    dedge,
+    dtail,
+    dgain,
+    dcum_row,
+    dskip,
+    dstate,
+):
+    @pl.when(pl.program_id(0) == 0)
+    def _():
+        dstate[...] = jnp.zeros_like(dstate)
+
+    keys = b[...].astype(jnp.bfloat16)
+    queries = c[...].astype(jnp.bfloat16)
+    scores = contract_cols(queries, keys)
+    mask = block_mask(seg_col, seg_row)
+    low_lane = lax.broadcasted_iota(jnp.int32, (BLOCK, 128), 1) < 64
+    dscores = jnp.zeros((BLOCK, BLOCK), jnp.float32)
+    dqueries = jnp.zeros(c.shape, jnp.float32)
+    dkeys = jnp.zeros(b.shape, jnp.float32)
+
+    def put(ref, pair, product):
+        low_part = jnp.sum(jnp.where(low_lane, product, 0.0), axis=1, keepdims=True)
+        all_part = jnp.sum(product, axis=1, keepdims=True)
+        ref[:, 2 * pair : 2 * pair + 1] = low_part
+        ref[:, 2 * pair + 1 : 2 * pair + 2] = all_part - low_part
+
+    for pair in range(v.shape[1] // 128):
+        cols = slice(128 * pair, 128 * pair + 128)
+        values = v[:, cols]
+        grad = dy[:, cols]
+        step_pair = pick(step, pair, low_lane)
+        edge_pair = pick(edge, pair, low_lane)
+        tail_pair = pick(tail, pair, low_lane)
+        scaled = values * step_pair
+        scaled_low = scaled.astype(jnp.bfloat16)
+        grad_low = grad.astype(jnp.bfloat16)
+        inside = []
+        for side in range(2):
+            head = 2 * pair + side
+            gap = cum[:, head : head + 1] - cum_row[head : head + 1, :]
+            decay = jnp.exp(jnp.where(mask, gap, -1e30))
+            weight = scores * decay
+            own = low_lane if side == 0 else jnp.logical_not(low_lane)
+            dweight = contract_cols(jnp.where(own, grad, 0.0).astype(jnp.bfloat16), scaled_low)
+            dscores = dscores + dweight * decay
+            product = dweight * weight
+            dcum[:, head : head + 1] = jnp.sum(product, axis=1, keepdims=True)
+            dcum_row[head : head + 1, :] = jnp.sum(product, axis=0, keepdims=True)
+            inside.append(contract_rows(weight.astype(jnp.bfloat16), grad_low))
+        before = prior[:, cols]
+        before_low = before.astype(jnp.bfloat16)
+        after = dstate[:, cols]
+        after_low = after.astype(jnp.bfloat16)
+        put(dedge, pair, grad * dot_rows(queries, before_low))
+        key_part = dot_rows(keys, after_low)
+        put(dtail, pair, scaled * key_part)
+        dscaled = jnp.where(low_lane, inside[0], inside[1]) + tail_pair * key_part
+        put(dstep, pair, dscaled * values)
+        dv[:, cols] = step_pair * dscaled + skip[:, cols] * grad
+        dgain[0, :, cols] = jnp.sum(before * after, axis=0, keepdims=True)
+        dskip[0, :, cols] = jnp.sum(grad * values, axis=0, keepdims=True)
+        edge_grad = (edge_pair * grad).astype(jnp.bfloat16)
+        dqueries = dqueries + contract_cols(edge_grad, before_low)
+        dkeys = dkeys + contract_cols((tail_pair * scaled).astype(jnp.bfloat16), after_low)
+        dstate[:, cols] = gain[0, :, cols] * after + contract_rows(queries, edge_grad)
+    dscores_low = dscores.astype(jnp.bfloat16)
+    dc[...] = dqueries + dot_rows(dscores_low, keys)
+    db[...] = dkeys + contract_rows(dscores_low, queries)
+
+
+def scan_specs(rows, width, heads, states, turned):
+    blocks = rows // BLOCK
+
+    def at(position):
+        return blocks - 1 - position if turned else position
+
+    wide = pl.BlockSpec((BLOCK, width), lambda i: (at(i), 0))
+    key = pl.BlockSpec((BLOCK, states), lambda i: (at(i), 0))
+    head = pl.BlockSpec((BLOCK, heads), lambda i: (at(i), 0))
+    line = pl.BlockSpec((1, 1, width), lambda i: (at(i), 0, 0))
+    across = pl.BlockSpec((heads, BLOCK), lambda i: (0, at(i)))
+    seg_col = pl.BlockSpec((BLOCK, 1), lambda i: (at(i), 0))
+    seg_row = pl.BlockSpec((1, BLOCK), lambda i: (0, at(i)))
+    fixed = pl.BlockSpec((1, width), lambda i: (0, 0))
+    prior = pl.BlockSpec((states, width), lambda i: (at(i), 0))
+    inputs = [wide, key, key, head, head, head, head, line, across, seg_col, seg_row, fixed]
+    return inputs, wide, key, head, line, across, prior
+
+
+def f32(*shape):
+    return jax.ShapeDtypeStruct(shape, jnp.float32)
+
+
+def scan_forward(parts, extra):
+    rows, width = parts[0].shape
+    states, heads = parts[1].shape[1], parts[3].shape[1]
+    blocks = rows // BLOCK
+    inputs, wide, key, head, line, across, prior = scan_specs(rows, width, heads, states, False)
+    return pl.pallas_call(
+        scan_forward_kernel,
+        grid=(blocks,),
+        in_specs=inputs,
+        out_specs=[wide, prior],
+        out_shape=[f32(rows, width), f32(blocks * states, width)],
+        scratch_shapes=[pltpu.VMEM((states, width), jnp.float32)],
+        compiler_params=pltpu.CompilerParams(vmem_limit_bytes=48 * 1024 * 1024),
+        name="scan_forward",
+    )(*parts, *extra)
+
+
+def scan_backward(parts, extra, grad_mixed, prior_states):
+    rows, width = parts[0].shape
+    states, heads = parts[1].shape[1], parts[3].shape[1]
+    blocks = rows // BLOCK
+    inputs, wide, key, head, line, across, prior = scan_specs(rows, width, heads, states, True)
+    return pl.pallas_call(
+        scan_backward_kernel,
+        grid=(blocks,),
+        in_specs=inputs + [wide, prior],
+        out_specs=[wide, key, key, head, head, head, head, line, across, line],
+        out_shape=[
+            f32(rows, width),
+            f32(rows, states),
+            f32(rows, states),
+            f32(rows, heads),
+            f32(rows, heads),
+            f32(rows, heads),
+            f32(rows, heads),
+            f32(blocks, 1, width),
+            f32(heads, rows),
+            f32(blocks, 1, width),
+        ],
+        scratch_shapes=[pltpu.VMEM((states, width), jnp.float32)],
+        compiler_params=pltpu.CompilerParams(vmem_limit_bytes=48 * 1024 * 1024),
+        name="scan_backward",
+    )(*parts, *extra, grad_mixed, prior_states)
+
+
+def dot_rows(left_side, right_side):
+    return jnp.dot(left_side, right_side, preferred_element_type=jnp.float32)
 
 
 def contract_rows(left_side, right_side):
@@ -187,8 +360,8 @@
     gate_z = jnp.dot(normed_all, gate_weight, preferred_element_type=jnp.float32)
     segment, present = segments(sequence_lengths, sequence_owner, device_index, row_count)
     present_float = present.astype(jnp.float32)
-    mixed_out, mixer_back = jax.vjp(
-        jax.checkpoint(partial(mixer, segment=segment)),
+    parts, prepare_back = jax.vjp(
+        partial(prepare, segment=segment),
         value_proj,
         bc_proj,
         step_raw,
@@ -198,8 +371,14 @@
         conv_bc_bias,
         step_bias,
         decay_log,
-        skip_gain,
-    )
+    )
+    extra = (
+        parts[4].T,
+        segment[:, None],
+        segment[None, :],
+        jnp.repeat(skip_gain, inner_local // heads_local)[None, :],
+    )
+    mixed_out, prior_states = scan_forward(parts, extra)
     gate_sigmoid = jax.nn.sigmoid(gate_z)
     silu_gate = gate_z * gate_sigmoid
     gated_out = mixed_out * silu_gate
@@ -227,6 +406,8 @@
     )
     grad_mixed = grad_gated * silu_gate
     grad_gate_z = grad_gated * mixed_out * gate_sigmoid * (1.0 + gate_z * (1.0 - gate_sigmoid))
+    *part_grads, dcum_row, dskip = scan_backward(parts, extra, grad_mixed, prior_states)
+    part_grads[4] = part_grads[4] - dcum_row.T
     (
         grad_value,
         grad_bc_part,
@@ -237,8 +418,8 @@
         g_conv_bc_bias,
         g_step_bias,
         g_decay_log,
-        g_skip_gain,
-    ) = mixer_back(grad_mixed)
+    ) = prepare_back(tuple(part_grads))
+    g_skip_gain = jnp.sum(dskip.reshape(-1, heads_local, inner_local // heads_local), axis=(0, 2))
     grad_gate_z = grad_gate_z.astype(jnp.bfloat16)
     early = jnp.concatenate(
         [contract_rows(normed_all, grad_gate_z), contract_rows(masked_cot, gnorm)], 1

time: 716 us -> 581 us (0.81)
  matrix products: 167 us -> 67.1 us
  Pallas kernels: 0 us -> 75.7 us
  other arithmetic: 182 us -> 122 us
  local copies, waits for them, and re-layouts: 103 us -> 54.5 us
    dot_general x18 -> x2, matrix products: 95.3 us -> 1.92 us  [prepare(): jnp.einsum('ij,cjh->cih', lower_mask.astype(jnp.float32), rates, precisio...]
    pallas_call x0 -> x2, Pallas kernels: none -> 75.7 us  [the longest x1 55.3 us: scan_backward(): pl.pallas_call(scan_backward_kernel, grid=(blocks,), in_specs=inputs + [w...]
    unnamed x320 -> x198, local copies, waits for them, and re-layouts: 47.3 us -> 17.2 us
    mul x9 -> x7, other arithmetic: 10.9 us -> 38.6 us  [the longest x1 16.5 us: prepare(): jax.nn.silu(conv_seq(value_proj, conv_value, conv_value_bias, segment))]
    add x16 -> x0, other arithmetic: 17.6 us -> none  [advance(): return (gain_now[:, None, None] * carry_state + fresh_state, carry_state)]
    reduce_sum x12 -> x5, other arithmetic: 21 us -> 3.61 us  [the longest x1 2.63 us: prepare(): step_size = jax.nn.softplus(step_raw + step_bias)]
    convert_element_type x3 -> x1, other arithmetic: 17.4 us -> 0.07 us  [prepare(): tail_mask = (segment_blocks == segment_blocks[:, -1:]).astype(jnp.float32)]
    dynamic_update_slice x24 -> x0, other arithmetic: 12.5 us -> none  [scan_heads(): lax.scan(advance, jnp.zeros((head_count, head_dim, state_size), jnp.float...]
  transfers between devices with their start and end apart: 9 -> 9, of which waited for: 5 -> 5; matrix products, arithmetic and copies ran while one was open for 29% -> 33% of each run, Pallas kernels for 0% -> 4%
where the time goes in v2:
time: 581 us; the launch traced here: 573 us
  waiting for transfers between devices  175 us (30%)
  other arithmetic  122 us (21%)
  Pallas kernels  75.7 us (13%)
  matrix products  67.1 us (12%)
  blocking collectives  62.3 us (11%)
  local copies, waits for them, and re-layouts  54.5 us (9%)
  between operations  15.5 us (3%)
    unnamed x11, waiting for transfers between devices  68.4 us
    pallas_call x1, Pallas kernels, scan_backward(): pl.pallas_call(scan_backward_kernel, grid=(blocks,), in_specs=inputs + [w...  55.3 us
    all_gather x1, waiting for transfers between devices, body(): normed_all = lax.all_gather(normed, 'tensor', axis=0, tiled=True)  45.7 us
    psum x1, blocking collectives, body(): lax.psum((gain_part, g_conv_bc, g_conv_bc_bias, widen(g_conv_value, tenso...  41.2 us
    all_gather x1, waiting for transfers between devices, body(): side_weight = lax.all_gather(side_pack, 'dp', axis=0, tiled=True)  32.1 us
    reduce_scatter x1, waiting for transfers between devices, body(): lax.psum_scatter((contract_cols(grad_gate_z, gate_weight) + contract_cols...  29.2 us
    reduce_sum x4, other arithmetic, conv_seq(): kernel[kernel_size - 1 - offset] * moved  28 us
    dot_general x4, matrix products, contract_cols(): lax.dot_general(left_side, right_side, (((1,), (1,)), ((), ())), preferre...  21.7 us
  transfers between devices with their start and end apart: 9, of which 5 were waited for; matrix products, arithmetic and copies ran while one was open for 33% of the time, Pallas kernels for 4%

profile of v2, /device:TPU:0, one launch (start us, length us, event | category | flops | bytes accessed | tf_op | source)
XLA Modules:
  0.0 573.5 jit_solution(14216716631159145937)
XLA Ops:
  9.7 1.8 fusion.15
  12.2 3.0 fusion.8
  21.7 32.1 %all-gather.7.cloned.1.call-done = bf16[768,1036]{1,0:T(8,128)(2,1)} async-done(((bf16[48,1036]{1,0:T(8,128)(2,1)}), bf16[768,1036]{1,0:T(8,128)(2,1)}) %all-gather.7.cloned.1.call-update) | async-done | bytes 1591312 | tf_op jit(solution)/shard_map/all_gather | solution.py:351
  53.8 45.7 %all-gather.5.cloned.1.call-done = bf16[2048,768]{1,0:T(8,128)(2,1)} async-done(((bf16[1024,768]{1,0:T(8,128)(2,1)}), bf16[2048,768]{1,0:T(8,128)(2,1)}) %all-gather.5.cloned.1.call-update) | async-done | bytes 3145744 | tf_op jit(solution)/shard_map/all_gather | solution.py:355
  99.6 6.7 %fusion.80 = f32[2048,1036]{1,0:T(8,128)S(1)} fusion(bf16[2048,768]{1,0:T(8,128)(2,1)} %all-gather.5.cloned.1.call-done, bf16[768,1036]{1,0:T(8,128)(2,1)} %all-gather.7.cloned.1.call-done), kind=kOutput, calls=%fused_computation.169 | convolution fusion | flops 3258974208 | bytes 13223936 | tf_op jit(solution)/shard_map/dot_general | solution.py:356
  106.3 2.3 slice.171
  109.2 2.5 slice.169
  115.5 5.6 fusion.25
  124.3 3.1 slice.166
  127.4 3.1 slice.164
  130.6 3.2 slice.162
  134.5 2.8 copy.226
  137.6 16.5 %fusion.3 = (f32[2048,768]{1,0:T(8,128)}, f32[2048,768]{1,0:T(8,128)}) fusion(f32[2048]{0:T(1024)S(1)} %get-tuple-element.203, f32[2045,768]{1,0:T(8,128)} %slice.166, f32[768]{0:T(1024)S(1)} %get-tuple-element.146, f32[2048]{0:T(1024)S(1)} %get-tuple-element.204, f32[2046,768]{1,0:T(8,128)} %slice.164, f32[768]{0:T(1024)S(1)} %get-tuple-element.147, ...), kind=kLoop, calls=%fused_computation.21 | loop fusion | flops 23592960 | bytes 37770240 | tf_op jit(solution)/shard_map/jvp(jit(silu))/mul | solution.py:55
  154.1 20.4 %scan_forward.1 = (f32[2048,768]{1,0:T(8,128)}, f32[1024,768]{1,0:T(8,128)}) custom-call(f32[2048,768]{1,0:T(8,128)} %get-tuple-element.179.v, f32[2048,128]{1,0:T(8,128)S(1)} %copy-done.5, f32[2048,128]{1,0:T(8,128)S(1)} %copy-done.4, f32[2048,12]{1,0:T(8,128)S(1)} %get-tuple-element.176.step, f32[2048,12]{1,0:T(8,128)S(1)} %copy.227.cum, ...), custom_call_target="tpu_custom_call" | custom-call | tf_op jit(solution)/shard_map/scan_forward/pallas_call | solution.py:246
  174.5 12.0 %multiply_reduce_fusion.6 = (f32[2048]{0:T(1024)S(1)}, f32[2048,768]{1,0:T(8,128)}, f32[2048,768]{1,0:T(8,128)}) fusion(f32[2048,768]{1,0:T(8,128)} %get-tuple-element.28, bf16[2048,768]{1,0:T(8,128)(2,1)} %all-gather.5.cloned.1.call-done, bf16[768,1536]{1,0:T(8,128)(2,1)} %all-gather.9.cloned.1.call-done), kind=kOutput, calls=%fused_computation.17 | convolution fusion | flops 2426927104 | bytes 23207936 | tf_op jit(solution)/shard_map/dot_general | solution.py:360
  186.6 5.0 psum.84
  191.6 8.4 %multiply_reduce_fusion = (f32[768]{0:T(1024)}, f32[2048]{0:T(1024)S(1)}, f32[2048,768]{1,0:T(8,128)}) fusion(f32[2048,768]{1,0:T(8,128)} %get-tuple-element.174, f32[2048]{0:T(1024)S(1)} %get-tuple-element.197, f32[768]{0:T(1024)S(1)} %copy-done.61, bf16[768,1536]{1,0:T(8,128)(2,1)} %all-gather.9.cloned.1.call-done, ...), kind=kOutput, calls=%fused_computation.6 | convolution fusion | flops 2426926336 | bytes 16934912 | tf_op jit(solution)/shard_map/dot_general | solution.py:398
  200.0 5.0 psum.85
  205.0 14.2 %fusion.17 = (f32[2048,768]{1,0:T(8,128)}, bf16[2048,768]{1,0:T(8,128)(2,1)}) fusion(f32[2048]{0:T(1024)S(1)} %broadcast_multiply_fusion.7, f32[2048,768]{1,0:T(8,128)} %get-tuple-element.174, f32[2048,768]{1,0:T(8,128)} %get-tuple-element.210, f32[2048]{0:T(1024)S(1)} %get-tuple-element.196, f32[768]{0:T(1024)S(1)} %copy-done.61, ...), kind=kLoop, calls=%fused_computation.43 | loop fusion | flops 26738688 | bytes 34630656 | tf_op jit(solution)/shard_map/mul | solution.py:407
  219.2 55.3 %scan_backward.1 = (f32[2048,768]{1,0:T(8,128)}, f32[2048,128]{1,0:T(8,128)S(1)}, f32[2048,128]{1,0:T(8,128)S(1)}, f32[2048,12]{1,0:T(8,128)S(1)}, f32[2048,12]{...) custom-call(f32[2048,768]{1,0:T(8,128)} %get-tuple-element.179.v, ...), custom_call_target="tpu_custom_call" | custom-call | tf_op jit(solution)/shard_map/scan_backward/pallas_call | solution.py:263
  274.5 2.8 multiply_reduce_fusion.10
  277.5 3.1 multiply_reduce_fusion.9
  284.8 3.8 fusion.45
  291.0 1.8 slice_multiply_fusion.4
  295.1 3.8 fusion.71
  299.0 11.7 %multiply_reduce_fusion.4 = (f32[768]{0:T(1024)S(1)}, f32[2048,768]{1,0:T(8,128)}, f32[2048,768]{1,0:T(8,128)}) fusion(f32[2045,768]{1,0:T(8,128)} %slice.166, f32[2048]{0:T(1024)S(1)} %get-tuple-element.203, f32[2048,768]{1,0:T(8,128)} %get-tuple-element.180, f32[2048,768]{1,0:T(8,128)} %get-tuple-element.30), kind=kLoop, calls=%fused_computation.10 | loop fusion | flops 18873600 | bytes 31459328 | tf_op jit(solution)/shard_map/transpose(jvp())/reduce_sum | solution.py:36
  310.7 6.0 %fusion.29 = bf16[768,768]{0,1:T(8,128)(2,1)S(1)} fusion(bf16[2048,768]{1,0:T(8,128)(2,1)S(1)} %copy-done.81, bf16[2048]{0:T(1024)(128)(2,1)S(1)} %copy-done.67, f32[2048,768]{1,0:T(8,128)} %get-tuple-element.174, f32[768]{0:T(1024)S(1)} %copy-done.62, f32[2048]{0:T(1024)S(1)} %copy-done.47), kind=kOutput, calls=%fused_computation.73 | convolution fusion | flops 2422800384 | bytes 10632192 | tf_op jit(solution)/shard_map/dot_general | solution.py:291
  316.8 2.9 convolution_convert_fusion.1
  321.2 4.4 copy.250
  325.7 2.6 fusion.72
  328.3 10.3 %multiply_reduce_fusion.3 = (f32[768]{0:T(1024)S(1)}, f32[2048,768]{1,0:T(8,128)S(1)}, f32[768]{0:T(1024)S(1)}, f32[2048,768]{1,0:T(8,128)}) fusion(f32[2046,768]{1,0:T(8,128)} %slice.164, f32[2048,768]{1,0:T(8,128)} %get-tuple-element.168, f32[2048]{0:T(1024)S(1)} %copy-done.33, f32[2047,768]{1,0:T(8,128)} %slice.162, f32[2048]{0:T(1024)S(1)} %get-tuple-element.202), kind=kLoop, calls=%fused_computation.9 | loop fusion | flops 9435648 | bytes 31470592 | tf_op jit(solution)/shard_map/transpose(jvp())/reduce_sum | solution.py:36
  338.6 3.3 slice_multiply_fusion.1
  342.2 6.8 %slice_multiply_fusion = f32[2047,768]{1,0:T(8,128)} fusion(f32[2048,768]{1,0:T(8,128)} %get-tuple-element.185, f32[768]{0:T(1024)S(1)} %copy-done.41), kind=kLoop, calls=%fused_computation.3 | loop fusion | flops 1572096 | bytes 12579840 | tf_op jit(solution)/shard_map/transpose(jvp())/mul | solution.py:36
  349.0 7.1 %slice_multiply_fusion.2 = f32[2045,768]{1,0:T(8,128)} fusion(f32[2048,768]{1,0:T(8,128)} %get-tuple-element.167, f32[768]{0:T(1024)S(1)} %copy-done.39), kind=kLoop, calls=%fused_computation.5 | loop fusion | flops 1570560 | bytes 12567552 | tf_op jit(solution)/shard_map/transpose(jvp())/mul | solution.py:36
  356.2 9.7 %fusion.70 = (f32[768]{0:T(1024)S(1)}, f32[768]{0:T(1024)S(1)}, bf16[2048,768]{1,0:T(8,128)(2,1)}) fusion(f32[2048,768]{1,0:T(8,128)S(1)} %bitcast.107, f32[2048,1036]{1,0:T(8,128)S(1)} %bitcast.105, f32[768]{0:T(1024)S(1)} %copy-done.37, f32[2047,768]{1,0:T(8,128)} %slice_multiply_fusion, f32[2046,768]{1,0:T(8,128)} %slice_multiply_fusion.1, ...), kind=kLoop, calls=%fused_computation.163 | loop fusion | flops 12581376 | bytes 34593792 | tf_op jit(solution)/shard_map/transpose(jvp())/reduce_sum | solution.py:30
  365.9 5.7 fusion.28
  371.6 1.7 convolution_convert_fusion.2
  373.4 2.3 copy.252
  375.8 5.0 fusion.48
  380.9 4.9 add_convert_fusion
  387.5 7.1 %convolution_convert_fusion = bf16[2048,768]{1,0:T(8,128)(2,1)} fusion(bf16[768,1536]{1,0:T(8,128)(2,1)S(1)} %copy-done.82, f32[2048,768]{1,0:T(8,128)} %get-tuple-element.174, f32[768]{0:T(1024)S(1)} %copy-done.62, f32[2048]{0:T(1024)S(1)} %copy-done.47), kind=kOutput, calls=%fused_computation.31 | convolution fusion | flops 2422210560 | bytes 10629120 | tf_op jit(solution)/shard_map/dot_general | solution.py:297
  396.8 7.6 %reduce-scatter.16.cloned.1.call-done = bf16[48,1536]{1,0:T(8,128)(2,1)} async-done(((bf16[768,1536]{1,0:T(8,128)(2,1)}), bf16[48,1536]{1,0:T(8,128)(2,1)}) %reduce-scatter.16.cloned.1.call-update) | async-done | bytes 147472
  407.3 60.1 %reduce-scatter.18.cloned.1.call-done = bf16[48,1036]{1,0:T(8,128)(2,1)} async-done(((bf16[768,1036]{1,0:T(8,128)(2,1)}), bf16[48,1036]{1,0:T(8,128)(2,1)}) %reduce-scatter.18.cloned.1.call-update) | async-done | bytes 99472
  469.8 11.1 %psum.87 = f32[48,256]{0,1:T(8,128)S(1)} all-reduce(f32[48,256]{0,1:T(8,128)S(1)} %copy.279), channel_id=1, replica_groups=mesh['dp'=16,'tensor'=2] {'tensor'}, use_global_device_ids=true, to_apply=%region_17.18 | all-reduce | flops 12288 | bytes 98304 | tf_op jit(solution)/shard_map/psum | solution.py:449
  483.5 29.2 %reduce-scatter.12.cloned.1.call-done = bf16[1024,768]{1,0:T(8,128)(2,1)} async-done(((bf16[2048,768]{1,0:T(8,128)(2,1)}), bf16[1024,768]{1,0:T(8,128)(2,1)}) %reduce-scatter.12.cloned.1.call-update) | async-done | bytes 1572880 | tf_op jit(solution)/shard_map/reduce_scatter | solution.py:437
  512.7 4.7 fusion.14
  517.4 41.2 %all-reduce.26 = (f32[768]{0:T(1024)}, f32[4,1536]{1,0:T(4,128)S(1)}, f32[1536]{0:T(1024)S(1)}, f32[4,256]{1,0:T(4,128)}, f32[256]{0:T(256)}, /*index=5*/f32[24]...) all-reduce(f32[768]{0:T(1024)S(1)} %get-tuple-element.140, ...), channel_id=1, replica_groups=mesh['dp'=16,'tensor'=2] {'dp','tensor'}, use_global_device_ids=true, to_apply=%region_14.15 | all-reduce | flops 11336 | bytes 90688 | tf_op jit(solution)/shard_map/psum | solution.py:459
  562.3 4.2 fusion.13
  (313 shorter events, 44.1 us)
Async XLA Ops:
  7.2 46.7 %all-gather.7.cloned.1.call-start = ((), (), s32[]{:S(2)}) async-start(), calls=%async_computation.6 | async-start | bytes 1880064 | tf_op jit(solution)/shard_map/all_gather | solution.py:351
  9.7 89.9 %all-gather.5.cloned.1.call-start = ((), (), s32[]{:S(2)}) async-start(), calls=%async_computation.5 | async-start | bytes 4718592 | tf_op jit(solution)/shard_map/all_gather | solution.py:355
  15.2 159.3 %all-gather.9.cloned.1.call-start = ((), (), s32[]{:S(2)}) async-start(), calls=%async_computation.7 | async-start | bytes 2506752 | tf_op jit(solution)/shard_map/all_gather | solution.py:352
  16.0 175.6 %all-gather.11.cloned.1.call-start = ((), (), s32[]{:S(2)}) async-start(), calls=%async_computation.9 | async-start | bytes 4718592 | tf_op jit(solution)/shard_map/all_gather | solution.py:397
  16.6 355.0 %reduce-scatter.14.cloned.1.call-start = ((), (), s32[]{:S(2)}) async-start(), calls=%async_computation.11 | async-start | bytes 1572864 | tf_op jit(solution)/shard_map/reduce_scatter | solution.py:428
  18.0 93.8 %copy-start.72 = (f32[12]{0:T(128)}, f32[12]{0:T(128)S(1)}, u32[]{:S(2)}) copy-start(f32[12]{0:T(128)S(1)} %exponential_negate_fusion) | copy-start | bytes 148
  18.0 97.4 %copy-start.51 = (f32[1,256]{1,0:T(1,128)}, f32[1,256]{1,0:T(1,128)S(1)}, u32[]{:S(2)}) copy-start(f32[1,256]{1,0:T(1,128)S(1)} %get-tuple-element.205) | copy-start | bytes 3076
  18.0 97.4 %copy-start.53 = (f32[1,256]{1,0:T(1,128)}, f32[1,256]{1,0:T(1,128)S(1)}, u32[]{:S(2)}) copy-start(f32[1,256]{1,0:T(1,128)S(1)} %get-tuple-element.207) | copy-start | bytes 3076
  18.0 97.4 %copy-start.55 = (f32[1,256]{1,0:T(1,128)}, f32[1,256]{1,0:T(1,128)S(1)}, u32[]{:S(2)}) copy-start(f32[1,256]{1,0:T(1,128)S(1)} %get-tuple-element.206) | copy-start | bytes 3076
  18.0 97.4 %copy-start.57 = (f32[1,256]{1,0:T(1,128)}, f32[1,256]{1,0:T(1,128)S(1)}, u32[]{:S(2)}) copy-start(f32[1,256]{1,0:T(1,128)S(1)} %get-tuple-element.208) | copy-start | bytes 3076
  18.9 172.7 %copy-start.66 = (bf16[2048]{0:T(1024)(128)(2,1)}, bf16[2048]{0:T(1024)(128)(2,1)S(1)}, u32[]{:S(2)}) copy-start(bf16[2048]{0:T(1024)(128)(2,1)S(1)} %fusion.65) | copy-start | bytes 12292
  18.9 118.6 %copy-start.36 = (f32[768]{0:T(1024)}, f32[768]{0:T(1024)S(1)}, u32[]{:S(2)}) copy-start(f32[768]{0:T(1024)S(1)} %get-tuple-element.144) | copy-start | bytes 9220
  18.9 118.6 %copy-start.38 = (f32[768]{0:T(1024)}, f32[768]{0:T(1024)S(1)}, u32[]{:S(2)}) copy-start(f32[768]{0:T(1024)S(1)} %get-tuple-element.146) | copy-start | bytes 9220
  18.9 118.6 %copy-start.40 = (f32[768]{0:T(1024)}, f32[768]{0:T(1024)S(1)}, u32[]{:S(2)}) copy-start(f32[768]{0:T(1024)S(1)} %get-tuple-element.145) | copy-start | bytes 9220
  19.0 118.6 %copy-start.42 = (f32[768]{0:T(1024)}, f32[768]{0:T(1024)S(1)}, u32[]{:S(2)}) copy-start(f32[768]{0:T(1024)S(1)} %get-tuple-element.147) | copy-start | bytes 9220
  19.3 103.3 %copy-start.25 = (f32[8,256]{0,1:T(8,128)}, f32[8,256]{0,1:T(8,128)S(1)}, u32[]{:S(2)}) copy-start(f32[8,256]{0,1:T(8,128)S(1)} %copy.225) | copy-start | bytes 24580
  21.6 102.6 %copy-start.59 = (f32[8]{0:T(128)}, f32[8]{0:T(128)S(1)}, u32[]{:S(2)}) copy-start(f32[8]{0:T(128)S(1)} %convert_reduce_fusion.1) | copy-start | bytes 100
  21.7 255.7 %copy-start.32 = (f32[2048]{0:T(1024)}, f32[2048]{0:T(1024)S(1)}, u32[]{:S(2)}) copy-start(f32[2048]{0:T(1024)S(1)} %get-tuple-element.204) | copy-start | bytes 24580
  112.4 41.6 %copy-start = (f32[2048,12]{1,0:T(8,128)}, f32[2048,12]{1,0:T(8,128)S(1)}, u32[]{:S(2)}) copy-start(f32[2048,12]{1,0:T(8,128)S(1)} %get-tuple-element.176.step) | copy-start | bytes 294916
  115.5 8.8 %slice-start = ((s8[9437184]{0:T(1024)(128)(4,1)}), s8[4194304]{0:T(1024)(128)(4,1)S(1)}, s32[]{:S(2)}) async-start(s8[9437184]{0:T(1024)(128)(4,1)} %bitcast.102), calls=%async_computation.14 | async-start | bytes 8388608
  115.5 8.8 %slice-start.1 = ((s8[9437184]{0:T(1024)(128)(4,1)}), s8[4194304]{0:T(1024)(128)(4,1)S(1)}, s32[]{:S(2)}) async-start(s8[9437184]{0:T(1024)(128)(4,1)} %bitcast.102), calls=%async_computation.15 | async-start | bytes 8388608
  134.4 19.6 %copy-start.2 = (f32[2048,12]{1,0:T(8,128)}, f32[2048,12]{1,0:T(8,128)S(1)}, u32[]{:S(2)}) copy-start(f32[2048,12]{1,0:T(8,128)S(1)} %copy.227.cum) | copy-start | bytes 294916
  137.5 16.6 %copy-start.3 = (f32[8,256,12]{2,1,0:T(8,128)}, f32[8,256,12]{2,1,0:T(8,128)S(1)}, u32[]{:S(2)}) copy-start(f32[8,256,12]{2,1,0:T(8,128)S(1)} %copy.224) | copy-start | bytes 294916
  137.5 16.5 %copy-start.4 = (f32[2048,128]{1,0:T(8,128)S(1)}, f32[2048,128]{1,0:T(8,128)}, u32[]{:S(2)}) copy-start(f32[2048,128]{1,0:T(8,128)} %get-tuple-element.190.c) | copy-start | bytes 3145732
  137.6 16.5 %copy-start.5 = (f32[2048,128]{1,0:T(8,128)S(1)}, f32[2048,128]{1,0:T(8,128)}, u32[]{:S(2)}) copy-start(f32[2048,128]{1,0:T(8,128)} %get-tuple-element.191.b) | copy-start | bytes 3145732
  174.5 17.1 %copy-start.61 = (f32[768]{0:T(1024)S(1)}, f32[768]{0:T(1024)}, u32[]{:S(2)}) copy-start(f32[768]{0:T(1024)} %param.35) | copy-start | bytes 9220
  191.5 13.4 %copy-start.46 = (f32[2048]{0:T(1024)}, f32[2048]{0:T(1024)S(1)}, u32[]{:S(2)}) copy-start(f32[2048]{0:T(1024)S(1)} %get-tuple-element.197) | copy-start | bytes 24580
  219.1 55.3 %copy-start.12 = (f32[2045,256]{1,0:T(8,128)S(1)}, f32[2045,256]{1,0:T(8,128)}, u32[]{:S(2)}) copy-start(f32[2045,256]{1,0:T(8,128)} %slice.171) | copy-start | bytes 6282244
  219.1 55.3 %copy-start.18 = (f32[2048,256]{1,0:T(8,128)S(1)}, f32[2048,256]{1,0:T(8,128)}, u32[]{:S(2)}) copy-start(f32[2048,256]{1,0:T(8,128)} %get-tuple-element.178) | copy-start | bytes 6291460
  298.9 105.6 %reduce-scatter.16.cloned.1.call-start = ((), (), s32[]{:S(2)}) async-start(), calls=%async_computation.12 | async-start | bytes 2506752
  298.9 11.8 %copy-start.47 = (f32[2048]{0:T(1024)S(1)}, f32[2048]{0:T(1024)}, u32[]{:S(2)}) copy-start(f32[2048]{0:T(1024)} %copy-done.46) | copy-start | bytes 24580
  298.9 11.8 %copy-start.62 = (f32[768]{0:T(1024)S(1)}, f32[768]{0:T(1024)}, u32[]{:S(2)}) copy-start(f32[768]{0:T(1024)} %param.35) | copy-start | bytes 9220
  299.0 11.8 %copy-start.67 = (bf16[2048]{0:T(1024)(128)(2,1)S(1)}, bf16[2048]{0:T(1024)(128)(2,1)}, u32[]{:S(2)}) copy-start(bf16[2048]{0:T(1024)(128)(2,1)} %copy-done.66) | copy-start | bytes 12292
  299.0 11.8 %copy-start.81 = (bf16[2048,768]{1,0:T(8,128)(2,1)S(1)}, bf16[2048,768]{1,0:T(8,128)(2,1)}, u32[]{:S(2)}) copy-start(bf16[2048,768]{1,0:T(8,128)(2,1)} %all-gather.11.cloned.1.call-done) | copy-start | bytes 9437188
  328.3 10.3 %copy-start.43 = (f32[768]{0:T(1024)S(1)}, f32[768]{0:T(1024)}, u32[]{:S(2)}) copy-start(f32[768]{0:T(1024)} %copy-done.42) | copy-start | bytes 9220
  341.9 125.6 %reduce-scatter.18.cloned.1.call-start = ((), (), s32[]{:S(2)}) async-start(), calls=%async_computation.13 | async-start | bytes 1880064
  342.2 13.9 %slice-start.3 = ((s8[9437184]{0:T(1024)(128)(4,1)}), s8[4194304]{0:T(1024)(128)(4,1)S(1)}, s32[]{:S(2)}) async-start(s8[9437184]{0:T(1024)(128)(4,1)} %bitcast.104), calls=%async_computation.17 | async-start | bytes 8388608
  342.2 13.9 %slice-start.4 = ((s8[9437184]{0:T(1024)(128)(4,1)}), s8[4194304]{0:T(1024)(128)(4,1)S(1)}, s32[]{:S(2)}) async-start(s8[9437184]{0:T(1024)(128)(4,1)} %bitcast.104), calls=%async_computation.18 | async-start | bytes 8388608
  342.2 13.9 %slice-start.6 = ((s8[6291456]{0:T(1024)(128)(4,1)}), s8[4194304]{0:T(1024)(128)(4,1)S(1)}, s32[]{:S(2)}) async-start(s8[6291456]{0:T(1024)(128)(4,1)} %bitcast.106), calls=%async_computation.20 | async-start | bytes 8388608
  356.2 9.7 %copy-start.30 = (bf16[2048,12]{1,0:T(8,128)(2,1)S(1)}, bf16[2048,12]{1,0:T(8,128)(2,1)}, u32[]{:S(2)}) copy-start(bf16[2048,12]{1,0:T(8,128)(2,1)} %get-tuple-element.158) | copy-start | bytes 147460
  375.8 136.9 %reduce-scatter.12.cloned.1.call-start = ((), (), s32[]{:S(2)}) async-start(), calls=%async_computation.10 | async-start | bytes 4718592 | tf_op jit(solution)/shard_map/reduce_scatter | solution.py:437
  385.9 176.5 %reduce-scatter.10.cloned.1.call-start = ((), (), s32[]{:S(2)}) async-start(), calls=%async_computation.8 | async-start | bytes 4718592 | tf_op jit(solution)/shard_map/reduce_scatter | solution.py:388
  395.3 88.2 %copy-start.48 = (f32[2048]{0:T(1024)}, f32[2048]{0:T(1024)S(1)}, u32[]{:S(2)}) copy-start(f32[2048]{0:T(1024)S(1)} %fusion.60) | copy-start | bytes 24580
  396.8 115.9 %copy-start.15 = (bf16[1024,768]{1,0:T(8,128)(2,1)S(1)}, bf16[1024,768]{1,0:T(8,128)(2,1)}, u32[]{:S(2)}) copy-start(bf16[1024,768]{1,0:T(8,128)(2,1)} %param.18) | copy-start | bytes 4718596
  396.8 115.9 %copy-start.45 = (f32[1024]{0:T(1024)S(1)}, f32[1024]{0:T(1024)}, u32[]{:S(2)}) copy-start(f32[1024]{0:T(1024)} %copy-done.44) | copy-start | bytes 12292
  396.8 115.9 %copy-start.49 = (f32[768]{0:T(1024)S(1)}, f32[768]{0:T(1024)}, u32[]{:S(2)}) copy-start(f32[768]{0:T(1024)} %param.22) | copy-start | bytes 9220
  483.5 78.8 %copy-start.20 = (bf16[1024,768]{1,0:T(8,128)(2,1)S(1)}, bf16[1024,768]{1,0:T(8,128)(2,1)}, u32[]{:S(2)}) copy-start(bf16[1024,768]{1,0:T(8,128)(2,1)} %param.19) | copy-start | bytes 4718596
  512.7 49.6 %dynamic-slice-start = ((f32[2048]{0:T(1024)}, s32[]{:T(128)}), f32[1024]{0:T(1024)S(1)}, s32[]{:S(2)}) async-start(f32[2048]{0:T(1024)} %copy-done.48, s32[]{:T(128)} %select_n.18), calls=%async_computation.22 | async-start | bytes 8704 | tf_op jit(solution)/shard_map/dynamic_slice | solution.py:394
  (54 other events, 221.0 us)
Sparse Core Ops, SparseCore 0:
  10.8 43.0 all-gather.6
  56.0 43.5 all-gather.4
  102.4 42.2 all-gather.8
  146.1 43.6 all-gather.10
  299.0 20.3 reduce-scatter.13
  342.0 62.4 reduce-scatter.15
  408.2 59.1 reduce-scatter.17
  469.7 42.9 reduce-scatter.11
  515.0 44.7 reduce-scatter.9

commit v3 on v2

--- a/solution.py
+++ b/solution.py
@@ -299,6 +299,24 @@
     )
 
 
+SWAP = ((0, 1), (1, 0))
+
+
+def swap_gather(own, tensor_index):
+    other = lax.ppermute(own, "tensor", SWAP)
+    first = jnp.where(tensor_index == 0, own, other)
+    second = jnp.where(tensor_index == 0, other, own)
+    return jnp.concatenate([first, second], 0)
+
+
+def swap_scatter(whole, tensor_index):
+    half = whole.shape[0] // 2
+    own = lax.dynamic_slice_in_dim(whole, tensor_index * half, half, 0)
+    away = lax.dynamic_slice_in_dim(whole, (1 - tensor_index) * half, half, 0)
+    other = lax.ppermute(away, "tensor", SWAP)
+    return (own.astype(jnp.float32) + other.astype(jnp.float32)).astype(jnp.bfloat16)
+
+
 def widen(local_part, tensor_count, tensor_index):
     axis_last = local_part.ndim - 1
     width_local = local_part.shape[axis_last]
@@ -352,7 +370,7 @@
     gate_pack = lax.all_gather(gate_pack, "dp", axis=0, tiled=True)
     gate_weight = gate_pack[:, :inner_local]
     out_weight = gate_pack[:, inner_local:]
-    normed_all = lax.all_gather(normed, "tensor", axis=0, tiled=True)
+    normed_all = swap_gather(normed, tensor_index)
     projected = jnp.dot(normed_all, side_weight, preferred_element_type=jnp.float32)
     value_proj = projected[:, :inner_local]
     step_raw = projected[:, inner_local : inner_local + heads_local]
@@ -385,16 +403,14 @@
     squares = lax.psum(jnp.sum(gated_out * gated_out, axis=-1), "tensor")
     gate_scale = lax.rsqrt(squares / inner_all + EPSILON)[:, None]
     gnorm = (gated_out * gate_scale * gate_gain).astype(jnp.bfloat16)
-    branch_own = lax.psum_scatter(
+    branch_own = swap_scatter(
         contract_cols(gnorm, out_weight).astype(jnp.bfloat16),
-        "tensor",
-        scatter_dimension=0,
-        tiled=True,
+        tensor_index,
     ).astype(jnp.float32)
     present_own = lax.dynamic_slice_in_dim(present_float, tensor_index * half_rows, half_rows, 0)
     block_out = (in_float + present_own[:, None] * branch_own).astype(jnp.bfloat16)
     mask_rows = present_float.astype(jnp.bfloat16)
-    masked_cot = lax.all_gather(cotangent, "tensor", axis=0, tiled=True) * mask_rows[:, None]
+    masked_cot = swap_gather(cotangent, tensor_index) * mask_rows[:, None]
     part_rows = jnp.dot(masked_cot, out_weight, preferred_element_type=jnp.float32)
     gated_scaled = gated_out * gate_scale
     grad_gate_gain = jnp.sum(part_rows * gated_scaled, axis=0)
@@ -425,23 +441,19 @@
         [contract_rows(normed_all, grad_gate_z), contract_rows(masked_cot, gnorm)], 1
     ).astype(jnp.bfloat16)
     early = lax.psum_scatter(early, "dp", scatter_dimension=0, tiled=True).astype(jnp.float32)
-    bc_own = lax.psum_scatter(
-        grad_bc_part.astype(jnp.bfloat16), "tensor", scatter_dimension=0, tiled=True
-    )
+    bc_own = swap_scatter(grad_bc_part.astype(jnp.bfloat16), tensor_index)
     grad_main = jnp.concatenate([grad_value, grad_step], 1).astype(jnp.bfloat16)
     late = jnp.concatenate(
         [contract_rows(normed_all, grad_main), contract_rows(normed, bc_own)], 1
     ).astype(jnp.bfloat16)
     late = lax.psum_scatter(late, "dp", scatter_dimension=0, tiled=True).astype(jnp.float32)
     side_cols = inner_local + heads_local
-    grad_normed = lax.psum_scatter(
+    grad_normed = swap_scatter(
         (
             contract_cols(grad_gate_z, gate_weight)
             + contract_cols(grad_main, side_weight[:, :side_cols])
         ).astype(jnp.bfloat16),
-        "tensor",
-        scatter_dimension=0,
-        tiled=True,
+        tensor_index,
     ).astype(jnp.float32) + contract_cols(bc_own, side_weight[:, side_cols:])
     summed = (
         early[:, :inner_local],

time: 581 us -> 511 us (0.88)
  waiting for transfers between devices: 175 us -> 85.9 us
  blocking collectives: 62.3 us -> 80.3 us
  other arithmetic: 122 us -> 114 us
  local copies, waits for them, and re-layouts: 54.5 us -> 60.9 us
    ppermute x0 -> x5, waiting for transfers between devices: none -> 85.9 us  [the longest x2 58.7 us: swap_gather(): other = lax.ppermute(own, 'tensor', SWAP)]
    unnamed x11 -> x6, waiting for transfers between devices: 68.4 us -> 0.07 us
    all_gather x2 -> x0, waiting for transfers between devices: 45.8 us -> none  [the longest x1 45.7 us: body(): normed_all = lax.all_gather(normed, 'tensor', axis=0, tiled=True)]
    all_gather x1, waiting for transfers between devices: 32.1 us -> 0.01 us  [body(): side_weight = lax.all_gather(side_pack, 'dp', axis=0, tiled=True)]
    reduce_scatter x3 -> x0, waiting for transfers between devices: 29.2 us -> none  [the longest x1 29.2 us: body(): lax.psum_scatter((contract_cols(grad_gate_z, gate_weight) + contract_cols...]
    psum x1, blocking collectives: 41.2 us -> 59.5 us  [body(): lax.psum((gain_part, g_conv_bc, g_conv_bc_bias, widen(g_conv_value, tenso...]
    mul x6, other arithmetic: 19.4 us -> 11.7 us  [conv_seq(): kernel[kernel_size - 1 - offset] * moved]
    select_n x0 -> x2, other arithmetic: none -> 7.19 us  [swap_gather(): first = jnp.where(tensor_index == 0, own, other)]
  transfers between devices with their start and end apart: 9 -> 9, of which waited for: 5 -> 3; matrix products, arithmetic and copies ran while one was open for 33% -> 35% of each run, Pallas kernels for 4% -> 4%
where the time goes in v3:
time: 511 us; the launch traced here: 501 us
  other arithmetic  114 us (22%)
  waiting for transfers between devices  85.9 us (17%)
  blocking collectives  80.3 us (16%)
  Pallas kernels  75.8 us (15%)
  matrix products  63.1 us (12%)
  local copies, waits for them, and re-layouts  60.9 us (12%)
  between operations  15.5 us (3%)
  starting transfers between devices  5.3 us (1%)
    psum x1, blocking collectives, body(): lax.psum((gain_part, g_conv_bc, g_conv_bc_bias, widen(g_conv_value, tenso...  59.5 us
    ppermute x2, waiting for transfers between devices, swap_gather(): other = lax.ppermute(own, 'tensor', SWAP)  58.7 us
    pallas_call x1, Pallas kernels, scan_backward(): pl.pallas_call(scan_backward_kernel, grid=(blocks,), in_specs=inputs + [w...  55.3 us
    ppermute x3, waiting for transfers between devices, swap_scatter(): other = lax.ppermute(away, 'tensor', SWAP)  27.2 us
    reduce_sum x4, other arithmetic, conv_seq(): kernel[kernel_size - 1 - offset] * moved  23.2 us
    unnamed x172, local copies, waits for them, and re-layouts  21.2 us
    pallas_call x1, Pallas kernels, scan_forward(): pl.pallas_call(scan_forward_kernel, grid=(blocks,), in_specs=inputs, out_...  20.5 us
    dot_general x4, matrix products, contract_cols(): lax.dot_general(left_side, right_side, (((1,), (1,)), ((), ())), preferre...  17.2 us
  transfers between devices with their start and end apart: 9, of which 3 were waited for; matrix products, arithmetic and copies ran while one was open for 35% of the time, Pallas kernels for 4%

profile of v3, /device:TPU:0, one launch (start us, length us, event | category | flops | bytes accessed | tf_op | source)
XLA Modules:
  0.0 501.2 jit_solution(8945136279458922887)
XLA Ops:
  11.9 3.0 fusion.8
  14.8 2.9 collective-permute-start
  23.6 29.7 %collective-permute-done = bf16[1024,768]{1,0:T(8,128)(2,1)} collective-permute-done((bf16[1024,768]{1,0:T(8,128)(2,1)}, bf16[1024,768]{1,0:T(8,128)(2,1)}, u32[]{:S(2)}, u32[]{:S(2)}) %collective-permute-start) | collective-permute-done | bytes 1572896 | tf_op jit(solution)/shard_map/ppermute | solution.py:306
  53.3 3.9 broadcast_select_fusion.3
  57.3 28.9 %collective-permute-done.2 = bf16[1024,768]{1,0:T(8,128)(2,1)} collective-permute-done((bf16[1024,768]{1,0:T(8,128)(2,1)S(1)}, bf16[1024,768]{1,0:T(8,128)(2,1)}, u32[]{:S(2)}, u32[]{:S(2)}) %collective-permute-start.2) | collective-permute-done | bytes 1572896 | tf_op jit(solution)/shard_map/ppermute | solution.py:306
  86.2 3.2 broadcast_select_fusion.1
  89.4 6.3 %fusion.73 = f32[2048,1036]{1,0:T(8,128)S(1)} fusion(bf16[768,1036]{1,0:T(8,128)(2,1)} %all-gather.3.cloned.1.call-done, bf16[1024,768]{1,0:T(8,128)(2,1)} %get-tuple-element.189, bf16[1024,768]{1,0:T(8,128)(2,1)S(1)} %copy-done.25), kind=kOutput, calls=%fused_computation.178 | convolution fusion | flops 3265265664 | bytes 13223936 | tf_op jit(solution)/shard_map/dot_general | solution.py:374
  95.8 2.3 slice.171
  98.1 2.6 slice.170
  100.7 2.0 slice.169
  102.7 3.1 slice.166
  105.8 3.1 slice.164
  108.9 3.2 slice.162
  119.1 5.9 %fusion.21 = (f32[2048,256]{1,0:T(8,128)S(1)}, f32[2048,256]{1,0:T(8,128)}) fusion(f32[2048]{0:T(1024)S(1)} %get-tuple-element.207, f32[2045,256]{1,0:T(8,128)} %slice.171, f32[256]{0:T(256)S(1)} %bitcast.118, f32[2048]{0:T(1024)S(1)} %get-tuple-element.208, f32[2046,256]{1,0:T(8,128)} %slice.170, f32[256]{0:T(256)S(1)} %bitcast.120, ...), kind=kLoop, calls=%fused_computation.67 | loop fusion | flops 7864320 | bytes 12606464 | tf_op jit(solution)/shard_map/jvp(jit(silu))/mul | solution.py:56
  125.7 14.7 %fusion.3 = (f32[2048,768]{1,0:T(8,128)}, f32[2048,768]{1,0:T(8,128)}) fusion(f32[2048]{0:T(1024)S(1)} %get-tuple-element.207, f32[2045,768]{1,0:T(8,128)S(1)} %bitcast.99, f32[768]{0:T(1024)S(1)} %get-tuple-element.146, f32[2048]{0:T(1024)S(1)} %get-tuple-element.208, f32[2046,768]{1,0:T(8,128)} %slice.164, f32[768]{0:T(1024)S(1)} %get-tuple-element.147, ...), kind=kLoop, calls=%fused_computation.21 | loop fusion | flops 23592960 | bytes 37770240 | tf_op jit(solution)/shard_map/jvp(jit(silu))/mul | solution.py:55
  140.5 20.5 %scan_forward.1 = (f32[2048,768]{1,0:T(8,128)}, f32[1024,768]{1,0:T(8,128)}) custom-call(f32[2048,768]{1,0:T(8,128)} %get-tuple-element.179.v, f32[2048,128]{1,0:T(8,128)S(1)} %get-tuple-element.195.b, f32[2048,128]{1,0:T(8,128)S(1)} %get-tuple-element.194.c, f32[2048,12]{1,0:T(8,128)S(1)} %get-tuple-element.176.step, f32[2048,12]{1,0:T(8,128)S(1)} %copy.227.cum, ...), custom_call_target="tpu_custom_call" | custom-call | tf_op jit(solution)/shard_map/scan_forward/pallas_call | solution.py:246
  161.0 12.2 %multiply_reduce_fusion.6 = (f32[2048]{0:T(1024)S(1)}, f32[2048,768]{1,0:T(8,128)}, f32[2048,768]{1,0:T(8,128)}) fusion(f32[2048,768]{1,0:T(8,128)} %get-tuple-element.28, bf16[768,1536]{1,0:T(8,128)(2,1)} %all-gather.5.cloned.1.call-done, bf16[1024,768]{1,0:T(8,128)(2,1)} %get-tuple-element.189, bf16[1024,768]{1,0:T(8,128)(2,1)} %get-tuple-element.188), kind=kOutput, calls=%fused_computation.17 | convolution fusion | flops 2433218560 | bytes 23207936 | tf_op jit(solution)/shard_map/dot_general | solution.py:378
  173.2 5.0 psum.84
  178.2 9.1 %multiply_reduce_fusion = (f32[768]{0:T(1024)}, f32[2048]{0:T(1024)S(1)}, f32[2048,768]{1,0:T(8,128)}) fusion(f32[2048,768]{1,0:T(8,128)} %get-tuple-element.174, f32[2048]{0:T(1024)S(1)} %get-tuple-element.201, f32[768]{0:T(1024)S(1)} %copy-done.50, bf16[768,1536]{1,0:T(8,128)(2,1)} %all-gather.5.cloned.1.call-done, ...), kind=kOutput, calls=%fused_computation.6 | convolution fusion | flops 2434790656 | bytes 16934912 | tf_op jit(solution)/shard_map/dot_general | solution.py:414
  187.3 5.0 psum.85
  192.3 14.1 %fusion.17 = (f32[2048,768]{1,0:T(8,128)}, bf16[2048,768]{1,0:T(8,128)(2,1)}) fusion(f32[2048]{0:T(1024)S(1)} %broadcast_multiply_fusion.7, f32[2048,768]{1,0:T(8,128)} %get-tuple-element.174, f32[2048,768]{1,0:T(8,128)} %get-tuple-element.214, f32[2048]{0:T(1024)S(1)} %get-tuple-element.200, f32[768]{0:T(1024)S(1)} %copy-done.50, ...), kind=kLoop, calls=%fused_computation.46 | loop fusion | flops 26738688 | bytes 34630656 | tf_op jit(solution)/shard_map/mul | solution.py:423
  206.4 55.3 %scan_backward.1 = (f32[2048,768]{1,0:T(8,128)}, f32[2048,128]{1,0:T(8,128)S(1)}, f32[2048,128]{1,0:T(8,128)S(1)}, f32[2048,12]{1,0:T(8,128)S(1)}, f32[2048,12]{...) custom-call(f32[2048,768]{1,0:T(8,128)} %get-tuple-element.179.v, ...), custom_call_target="tpu_custom_call" | custom-call | tf_op jit(solution)/shard_map/scan_backward/pallas_call | solution.py:263
  261.7 3.2 multiply_reduce_fusion.10
  267.8 3.2 fusion.75
  277.4 2.3 copy.238
  279.7 2.3 fusion.49
  283.8 3.8 fusion.41
  288.9 8.3 %multiply_reduce_fusion.4 = (f32[768]{0:T(1024)S(1)}, f32[2048,768]{1,0:T(8,128)S(1)}, f32[2048,768]{1,0:T(8,128)S(1)}) fusion(f32[2045,768]{1,0:T(8,128)} %slice.166, f32[2048]{0:T(1024)S(1)} %get-tuple-element.207, f32[2048,768]{1,0:T(8,128)} %get-tuple-element.180, f32[2048,768]{1,0:T(8,128)} %get-tuple-element.30), kind=kLoop, calls=%fused_computation.10 | loop fusion | flops 18873600 | bytes 31459328 | tf_op jit(solution)/shard_map/transpose(jvp())/reduce_sum | solution.py:36
  297.2 10.0 %multiply_reduce_fusion.3 = (f32[768]{0:T(1024)S(1)}, f32[2048,768]{1,0:T(8,128)}, f32[768]{0:T(1024)S(1)}, f32[2048,768]{1,0:T(8,128)S(1)}) fusion(f32[2046,768]{1,0:T(8,128)} %slice.164, f32[2048,768]{1,0:T(8,128)S(1)} %get-tuple-element.168, f32[2048]{0:T(1024)S(1)} %get-tuple-element.208, f32[2047,768]{1,0:T(8,128)} %slice.162, ...), kind=kLoop, calls=%fused_computation.9 | loop fusion | flops 9435648 | bytes 31470592 | tf_op jit(solution)/shard_map/transpose(jvp())/reduce_sum | solution.py:36
  307.2 3.8 slice_multiply_fusion
  312.2 3.8 slice_multiply_fusion.1
  316.1 3.4 slice_multiply_fusion.2
  319.7 9.5 %fusion.74 = (f32[768]{0:T(1024)S(1)}, f32[768]{0:T(1024)S(1)}, bf16[2048,768]{1,0:T(8,128)(2,1)S(1)}) fusion(f32[2048,768]{1,0:T(8,128)} %copy-done.7, f32[2048,1036]{1,0:T(8,128)S(1)} %bitcast.97, f32[768]{0:T(1024)S(1)} %get-tuple-element.144, f32[2047,768]{1,0:T(8,128)} %slice_multiply_fusion, f32[2046,768]{1,0:T(8,128)} %slice_multiply_fusion.1, ...), kind=kLoop, calls=%fused_computation.179 | loop fusion | flops 12581376 | bytes 34593792 | tf_op jit(solution)/shard_map/transpose(jvp())/reduce_sum | solution.py:30
  332.5 2.9 fusion.26
  335.4 2.2 convolution_convert_fusion.2
  337.8 2.2 copy.252
  340.1 5.2 %convolution_convert_fusion.1 = bf16[768,768]{0,1:T(8,128)(2,1)S(1)} fusion(bf16[2048,768]{1,0:T(8,128)(2,1)} %get-tuple-element.182, bf16[1024,768]{1,0:T(8,128)(2,1)} %get-tuple-element.189, bf16[1024,768]{1,0:T(8,128)(2,1)S(1)} %copy-done.27), kind=kOutput, calls=%fused_computation.79 | convolution fusion | flops 2422800384 | bytes 7471104 | tf_op jit(solution)/shard_map/dot_general | solution.py:291
  345.3 6.0 %fusion.27 = bf16[768,768]{0,1:T(8,128)(2,1)S(1)} fusion(bf16[1024,768]{1,0:T(8,128)(2,1)S(1)} %copy-done.31, bf16[1024,768]{1,0:T(8,128)(2,1)S(1)} %copy-done.30, bf16[2048]{0:T(1024)(128)(2,1)S(1)} %copy-done.57, f32[2048,768]{1,0:T(8,128)} %get-tuple-element.174, f32[768]{0:T(1024)S(1)} %copy-done.51, f32[2048]{0:T(1024)S(1)} %get-tuple-element.201), kind=kOutput, calls=%fused_computation.80 | convolution fusion | flops 2430664704 | bytes 10632192 | tf_op jit(solution)/shard_map/dot_general | solution.py:291
  351.5 2.8 copy.250
  354.4 5.1 %fusion.44 = f32[2048,768]{1,0:T(8,128)S(1)} fusion(bf16[2048,768]{1,0:T(8,128)(2,1)} %get-tuple-element.182, bf16[768,1536]{1,0:T(8,128)(2,1)} %all-gather.5.cloned.1.call-done), kind=kOutput, calls=%fused_computation.109 | convolution fusion | flops 2415919104 | bytes 10616832 | tf_op jit(solution)/shard_map/dot_general | solution.py:297
  359.6 3.7 add_convert_fusion
  364.7 1.9 copy-done.70
  366.7 2.9 convolution_convert_fusion
  375.0 27.2 %collective-permute-done.3 = bf16[1024,768]{1,0:T(8,128)(2,1)} collective-permute-done((bf16[1024,768]{1,0:T(8,128)(2,1)}, bf16[1024,768]{1,0:T(8,128)(2,1)}, u32[]{:S(2)}, u32[]{:S(2)}) %collective-permute-start.3) | collective-permute-done | bytes 1572896 | tf_op jit(solution)/shard_map/ppermute | solution.py:316
  402.2 5.5 %fusion.14 = (f32[768]{0:T(1024)S(1)}, f32[1024]{0:T(1024)S(1)}, f32[1024,768]{1,0:T(8,128)}) fusion(bf16[1024,768]{1,0:T(8,128)(2,1)S(1)} %copy-done.9, f32[1024]{0:T(1024)S(1)} %copy-done.39, f32[768]{0:T(1024)S(1)} %copy-done.41, bf16[768,1036]{1,0:T(8,128)(2,1)} %all-gather.3.cloned.1.call-done, bf16[1024,256]{1,0:T(8,128)(2,1)} %collective-permute-done.4, ...), kind=kOutput, calls=%fused_computation.38 | convolution fusion | flops 413923584 | bytes 9321472 | tf_op jit(solution)/shard_map/dot_general | solution.py:297
  407.7 59.5 %all-reduce.26 = (f32[768]{0:T(1024)}, f32[4,1536]{1,0:T(4,128)S(1)}, f32[1536]{0:T(1024)S(1)}, f32[4,256]{1,0:T(4,128)}, f32[256]{0:T(256)}, /*index=5*/f32[24]...) all-reduce(f32[768]{0:T(1024)S(1)} %get-tuple-element.140, ...), channel_id=1, replica_groups=mesh['dp'=16,'tensor'=2] {'dp','tensor'}, use_global_device_ids=true, to_apply=%region_11.12 | all-reduce | flops 11336 | bytes 90688 | tf_op jit(solution)/shard_map/psum | solution.py:471
  470.9 4.7 fusion.13
  478.4 10.9 %psum.87 = f32[48,256]{0,1:T(8,128)S(1)} all-reduce(f32[48,256]{0,1:T(8,128)S(1)} %copy.279), channel_id=1, replica_groups=mesh['dp'=16,'tensor'=2] {'tensor'}, use_global_device_ids=true, to_apply=%region_14.15 | all-reduce | flops 12288 | bytes 98304 | tf_op jit(solution)/shard_map/psum | solution.py:461
  (286 shorter events, 53.2 us)
Async XLA Ops:
  7.2 10.6 %copy-start.16 = (bf16[1024,768]{1,0:T(8,128)(2,1)S(1)}, bf16[1024,768]{1,0:T(8,128)(2,1)}, u32[]{:S(2)}) copy-start(bf16[1024,768]{1,0:T(8,128)(2,1)} %param.19) | copy-start | bytes 4718596
  7.2 10.6 %copy-start.36 = (bf16[768,48]{0,1:T(8,128)(2,1)S(1)}, bf16[768,48]{0,1:T(8,128)(2,1)}, u32[]{:S(2)}) copy-start(bf16[768,48]{0,1:T(8,128)(2,1)} %param.27) | copy-start | bytes 221188
  7.2 10.6 %copy-start.37 = (bf16[48,768]{1,0:T(8,128)(2,1)S(1)}, bf16[48,768]{1,0:T(8,128)(2,1)}, u32[]{:S(2)}) copy-start(bf16[48,768]{1,0:T(8,128)(2,1)} %param.23) | copy-start | bytes 221188
  7.2 11.4 %copy-start.67 = (s32[32]{0:T(128)S(1)}, s32[32]{0:T(128)}, u32[]{:S(2)}) copy-start(s32[32]{0:T(128)} %param.21) | copy-start | bytes 388
  7.2 11.4 %copy-start.66 = (s32[32]{0:T(128)S(1)}, s32[32]{0:T(128)}, u32[]{:S(2)}) copy-start(s32[32]{0:T(128)} %param.20) | copy-start | bytes 388
  7.2 82.2 %all-gather.3.cloned.1.call-start = ((), (), s32[]{:S(2)}) async-start(), calls=%async_computation.2 | async-start | bytes 1880064 | tf_op jit(solution)/shard_map/all_gather | solution.py:369
  9.8 12.5 %copy-start.65 = (f32[12]{0:T(128)S(1)}, f32[12]{0:T(128)}, u32[]{:S(2)}) copy-start(f32[12]{0:T(128)} %param.34) | copy-start | bytes 148
  9.8 13.5 %copy-start.42 = (f32[4,768]{1,0:T(4,128)S(1)}, f32[4,768]{1,0:T(4,128)}, u32[]{:S(2)}) copy-start(f32[4,768]{1,0:T(4,128)} %param.28) | copy-start | bytes 36868
  9.8 13.6 %copy-start.68 = (f32[12]{0:T(128)S(1)}, f32[12]{0:T(128)}, u32[]{:S(2)}) copy-start(f32[12]{0:T(128)} %param.33) | copy-start | bytes 148
  9.9 13.6 %copy-start.58 = (f32[4,256]{1,0:T(4,128)S(1)}, f32[4,256]{1,0:T(4,128)}, u32[]{:S(2)}) copy-start(f32[4,256]{1,0:T(4,128)} %param.30) | copy-start | bytes 12292
  9.9 43.5 %copy-start.8 = (bf16[1024,768]{1,0:T(8,128)(2,1)S(1)}, bf16[1024,768]{1,0:T(8,128)(2,1)}, u32[]{:S(2)}) copy-start(bf16[1024,768]{1,0:T(8,128)(2,1)} %param.18) | copy-start | bytes 4718596
  9.9 43.4 %copy-start.40 = (f32[768]{0:T(1024)S(1)}, f32[768]{0:T(1024)}, u32[]{:S(2)}) copy-start(f32[768]{0:T(1024)} %param.22) | copy-start | bytes 9220
  9.9 151.1 %all-gather.5.cloned.1.call-start = ((), (), s32[]{:S(2)}) async-start(), calls=%async_computation.3 | async-start | bytes 2506752 | tf_op jit(solution)/shard_map/all_gather | solution.py:370
  11.9 45.4 %copy-start.38 = (f32[1024]{0:T(1024)}, f32[1024]{0:T(1024)S(1)}, u32[]{:S(2)}) copy-start(f32[1024]{0:T(1024)S(1)} %add_rsqrt_fusion.1) | copy-start | bytes 12292
  14.8 38.5 %collective-permute-start = (bf16[1024,768]{1,0:T(8,128)(2,1)}, bf16[1024,768]{1,0:T(8,128)(2,1)}, u32[]{:S(2)}, u32[]{:S(2)}) collective-permute-start(bf16[1024,768]{1,0:T(8,128)(2,1)} %fusion.8), channel_id=1, source_target_pairs={{0,1},{1,0},{2,3},{3,2},{4,5},{5,4},{6,7},{7,6},{8,9},{9,8},{10,11... | collective-permute-start | bytes 4718600 | tf_op jit(solution)/shard_map/ppermute | solution.py:306
  17.8 68.4 %collective-permute-start.2 = (bf16[1024,768]{1,0:T(8,128)(2,1)S(1)}, bf16[1024,768]{1,0:T(8,128)(2,1)}, u32[]{:S(2)}, u32[]{:S(2)}) collective-permute-start(bf16[1024,768]{1,0:T(8,128)(2,1)S(1)} %copy-done.16), channel_id=1, source_target_pairs={{0,1},{1,0},{2,3},{3,2},{4,5},{5,4},{6,7},{7,6},{8,9},{9,8},{10,11... | collective-permute-start | bytes 4718600 | tf_op jit(solution)/shard_map/ppermute | solution.py:306
  18.5 457.1 %reduce-scatter.9.cloned.1.call-start = ((), (), s32[]{:S(2)}) async-start(), calls=%async_computation.5 | async-start | bytes 1880064
  20.2 94.5 %copy-start.23 = (f32[8,256]{0,1:T(8,128)}, f32[8,256]{0,1:T(8,128)S(1)}, u32[]{:S(2)}) copy-start(f32[8,256]{0,1:T(8,128)S(1)} %copy.225) | copy-start | bytes 24580
  23.2 155.0 %copy-start.56 = (bf16[2048]{0:T(1024)(128)(2,1)}, bf16[2048]{0:T(1024)(128)(2,1)S(1)}, u32[]{:S(2)}) copy-start(bf16[2048]{0:T(1024)(128)(2,1)S(1)} %fusion.64) | copy-start | bytes 12292
  23.4 94.7 %copy-start.47 = (f32[8]{0:T(128)}, f32[8]{0:T(128)S(1)}, u32[]{:S(2)}) copy-start(f32[8]{0:T(128)S(1)} %convert_reduce_fusion.1) | copy-start | bytes 100
  23.4 88.7 %copy-start.62 = (f32[12]{0:T(128)}, f32[12]{0:T(128)S(1)}, u32[]{:S(2)}) copy-start(f32[12]{0:T(128)S(1)} %exponential_negate_fusion) | copy-start | bytes 148
  23.5 95.6 %copy-start.43 = (f32[1,256]{1,0:T(1,128)}, f32[1,256]{1,0:T(1,128)S(1)}, u32[]{:S(2)}) copy-start(f32[1,256]{1,0:T(1,128)S(1)} %get-tuple-element.212) | copy-start | bytes 3076
  23.5 95.6 %copy-start.45 = (f32[1,256]{1,0:T(1,128)}, f32[1,256]{1,0:T(1,128)S(1)}, u32[]{:S(2)}) copy-start(f32[1,256]{1,0:T(1,128)S(1)} %get-tuple-element.210) | copy-start | bytes 3076
  57.3 32.2 %copy-start.25 = (bf16[1024,768]{1,0:T(8,128)(2,1)S(1)}, bf16[1024,768]{1,0:T(8,128)(2,1)}, u32[]{:S(2)}) copy-start(bf16[1024,768]{1,0:T(8,128)(2,1)} %get-tuple-element.188) | copy-start | bytes 4718596
  95.8 16.4 %copy-start.6 = (f32[2048,1036]{1,0:T(8,128)}, f32[2048,1036]{1,0:T(8,128)S(1)}, u32[]{:S(2)}) copy-start(f32[2048,1036]{1,0:T(8,128)S(1)} %fusion.73) | copy-start | bytes 25460740
  112.8 27.7 %copy-start = (f32[2048,12]{1,0:T(8,128)}, f32[2048,12]{1,0:T(8,128)S(1)}, u32[]{:S(2)}) copy-start(f32[2048,12]{1,0:T(8,128)S(1)} %get-tuple-element.176.step) | copy-start | bytes 294916
  114.7 25.8 %copy-start.2 = (f32[2048,12]{1,0:T(8,128)}, f32[2048,12]{1,0:T(8,128)S(1)}, u32[]{:S(2)}) copy-start(f32[2048,12]{1,0:T(8,128)S(1)} %copy.227.cum) | copy-start | bytes 294916
  116.8 23.7 %copy-start.3 = (f32[8,256,12]{2,1,0:T(8,128)}, f32[8,256,12]{2,1,0:T(8,128)S(1)}, u32[]{:S(2)}) copy-start(f32[8,256,12]{2,1,0:T(8,128)S(1)} %copy.224) | copy-start | bytes 294916
  125.2 15.4 %copy-start.4 = (f32[2048,128]{1,0:T(8,128)}, f32[2048,128]{1,0:T(8,128)S(1)}, u32[]{:S(2)}) copy-start(f32[2048,128]{1,0:T(8,128)S(1)} %get-tuple-element.194.c) | copy-start | bytes 3145732
  125.2 15.4 %copy-start.5 = (f32[2048,128]{1,0:T(8,128)}, f32[2048,128]{1,0:T(8,128)S(1)}, u32[]{:S(2)}) copy-start(f32[2048,128]{1,0:T(8,128)S(1)} %get-tuple-element.195.b) | copy-start | bytes 3145732
  161.0 17.2 %copy-start.29 = (bf16[1024,768]{1,0:T(8,128)(2,1)S(1)}, bf16[1024,768]{1,0:T(8,128)(2,1)}, u32[]{:S(2)}) copy-start(bf16[1024,768]{1,0:T(8,128)(2,1)} %get-tuple-element.186) | copy-start | bytes 4718596
  161.0 17.2 %copy-start.50 = (f32[768]{0:T(1024)S(1)}, f32[768]{0:T(1024)}, u32[]{:S(2)}) copy-start(f32[768]{0:T(1024)} %param.35) | copy-start | bytes 9220
  206.4 55.3 %copy-start.13 = (f32[2045,256]{1,0:T(8,128)S(1)}, f32[2045,256]{1,0:T(8,128)}, u32[]{:S(2)}) copy-start(f32[2045,256]{1,0:T(8,128)} %slice.171) | copy-start | bytes 6282244
  271.0 8.7 %copy-start.24 = (f32[8,256]{0,1:T(8,128)S(1)}, f32[8,256]{0,1:T(8,128)}, u32[]{:S(2)}) copy-start(f32[8,256]{0,1:T(8,128)} %copy-done.23) | copy-start | bytes 24580
  272.0 11.7 %copy-start.48 = (f32[8]{0:T(128)S(1)}, f32[8]{0:T(128)}, u32[]{:S(2)}) copy-start(f32[8]{0:T(128)} %copy-done.47) | copy-start | bytes 100
  272.8 62.6 %collective-permute-start.4 = (bf16[1024,256]{1,0:T(8,128)(2,1)}, bf16[1024,256]{1,0:T(8,128)(2,1)}, u32[]{:S(2)}, u32[]{:S(2)}) collective-permute-start(bf16[1024,256]{1,0:T(8,128)(2,1)} %constant_dynamic-slice_fusion.1), channel_id=1, source_target_pairs={{0,1},{1,0},{2,3},{3,2},{4,5},{5,4},{6,7},{7,6},{8,9},{9,8},{10,11... | collective-permute-start | bytes 1572872 | tf_op jit(solution)/shard_map/ppermute | solution.py:316
  297.2 10.0 %copy-start.7 = (f32[2048,768]{1,0:T(8,128)}, f32[2048,768]{1,0:T(8,128)S(1)}, u32[]{:S(2)}) copy-start(f32[2048,768]{1,0:T(8,128)S(1)} %get-tuple-element.168) | copy-start | bytes 18874372
  319.7 9.6 %copy-start.1 = (f32[2048,12]{1,0:T(8,128)S(1)}, f32[2048,12]{1,0:T(8,128)}, u32[]{:S(2)}) copy-start(f32[2048,12]{1,0:T(8,128)} %copy-done) | copy-start | bytes 294916
  319.7 9.6 %copy-start.61 = (f32[12]{0:T(128)S(1)}, f32[12]{0:T(128)}, u32[]{:S(2)}) copy-start(f32[12]{0:T(128)} %param.32) | copy-start | bytes 148
  319.7 9.6 %copy-start.63 = (f32[12]{0:T(128)S(1)}, f32[12]{0:T(128)}, u32[]{:S(2)}) copy-start(f32[12]{0:T(128)} %copy-done.62) | copy-start | bytes 148
  340.0 151.4 %reduce-scatter.7.cloned.1.call-start = ((), (), s32[]{:S(2)}) async-start(), calls=%async_computation.4 | async-start | bytes 2506752
  354.4 10.3 %slice-start.5 = ((s8[6291456]{0:T(1024)(128)(4,1)}), s8[4194304]{0:T(1024)(128)(4,1)S(1)}, s32[]{:S(2)}) async-start(s8[6291456]{0:T(1024)(128)(4,1)} %bitcast.105), calls=%async_computation.11 | async-start | bytes 8388608
  364.5 37.7 %collective-permute-start.3 = (bf16[1024,768]{1,0:T(8,128)(2,1)}, bf16[1024,768]{1,0:T(8,128)(2,1)}, u32[]{:S(2)}, u32[]{:S(2)}) collective-permute-start(bf16[1024,768]{1,0:T(8,128)(2,1)} %constant_dynamic-slice_fusion.2), channel_id=1, source_target_pairs={{0,1},{1,0},{2,3},{3,2},{4,5},{5,4},{6,7},{7,6},{8,9},{9,8},{10,11... | collective-permute-start | bytes 4718600 | tf_op jit(solution)/shard_map/ppermute | solution.py:316
  371.3 30.9 %copy-start.9 = (bf16[1024,768]{1,0:T(8,128)(2,1)S(1)}, bf16[1024,768]{1,0:T(8,128)(2,1)}, u32[]{:S(2)}) copy-start(bf16[1024,768]{1,0:T(8,128)(2,1)} %param.18) | copy-start | bytes 4718596
  371.4 30.8 %copy-start.39 = (f32[1024]{0:T(1024)S(1)}, f32[1024]{0:T(1024)}, u32[]{:S(2)}) copy-start(f32[1024]{0:T(1024)} %copy-done.38) | copy-start | bytes 12292
  371.4 30.8 %copy-start.41 = (f32[768]{0:T(1024)S(1)}, f32[768]{0:T(1024)}, u32[]{:S(2)}) copy-start(f32[768]{0:T(1024)} %param.22) | copy-start | bytes 9220
  372.6 98.2 %collective-permute-start.1 = (bf16[1024,768]{1,0:T(8,128)(2,1)}, bf16[1024,768]{1,0:T(8,128)(2,1)}, u32[]{:S(2)}, u32[]{:S(2)}) collective-permute-start(bf16[1024,768]{1,0:T(8,128)(2,1)} %constant_dynamic-slice_fusion.3), channel_id=1, source_target_pairs={{0,1},{1,0},{2,3},{3,2},{4,5},{5,4},{6,7},{7,6},{8,9},{9,8},{10,11... | collective-permute-start | bytes 4718600 | tf_op jit(solution)/shard_map/ppermute | solution.py:316
  375.0 95.9 %copy-start.17 = (bf16[1024,768]{1,0:T(8,128)(2,1)S(1)}, bf16[1024,768]{1,0:T(8,128)(2,1)}, u32[]{:S(2)}) copy-start(bf16[1024,768]{1,0:T(8,128)(2,1)} %param.19) | copy-start | bytes 4718596
  (40 other events, 167.7 us)
Sparse Core Ops, SparseCore 0:
  10.2 43.1 all-gather.2
  56.2 40.9 all-gather.4
  340.1 60.4 reduce-scatter.8
  404.2 62.1 reduce-scatter.6
